TPU v7x, 512 devices: a whole 4x8x8 slice. The times are simulated.
512 devices in a mesh: dp: 8 (over z), cls: 64 (over y, x, core).
Axes of the slice: x: 4, y: 8, z: 8, core: 2. Of those that a mesh axis runs over, the one named last changes fastest.
Arguments:
- features: bfloat16 [4096, 6144], P(('dp', 'cls')), may hold values from -112 to 112
- basis: bfloat16 [2048, 6144], P('cls'), may hold values from -0.078125 to 0.078125
- weights: bfloat16 [2048, 16384], P(None, 'cls'), may hold values from -0.125 to 0.125
- labels: int32 [4096], P('dp'), may hold values from 0 to 16383
Outputs:
- losses: float32 [2, 4096], P(None, 'dp')
- grad_total: float32 [2048, 16384], P('dp', 'cls')
All inputs are finite; a program needn't handle non-finite values.
Results may differ from a plain program's by a relative error of at most 0.014.
The roundings to bfloat16 on the way count: a program that leaves them out, or rounds other values in their place, can miss the bound.
Values may be sent and summed in bfloat16 or wider, within the bound.
No kernel may reach another device: no remote copies, remote signals or barrier semaphores. Data moves between devices by JAX's collectives and lax.ppermute only.
A program may use at most 64 MiB of HBM per device.

v0:
```python
import jax
import jax.numpy as jnp
from jax import lax
from jax.sharding import PartitionSpec as P

WHITE = 2048


STEP_SCALE = 2.0


def shards(features, basis, weights, labels):
    own_rows_white = lax.dot_general(
        basis,
        lax.all_gather(features, "cls", axis=0, tiled=True),
        (((1,), (1,)), ((), ())),
        preferred_element_type=jnp.float32,
    ).astype(jnp.bfloat16)
    white_t = lax.all_gather(own_rows_white, "cls", axis=0, tiled=True)
    width = weights.shape[1]
    class_ids = lax.axis_index("cls") * width + lax.iota(jnp.int32, width)
    target = labels[:, None] == class_ids[None, :]
    step_size = STEP_SCALE / WHITE

    def forward(current):
        logits = lax.dot_general(
            white_t, current, (((0,), (0,)), ((), ())), preferred_element_type=jnp.float32
        )
        picked = jnp.sum(jnp.where(target, logits, 0.0), axis=1)
        local_top = jnp.max(logits, axis=1)
        top = lax.pmax(local_top, "cls")
        local_total = jnp.sum(jnp.exp(logits - top[:, None]), axis=1)
        total, label_logit = lax.psum((local_total, picked), "cls")
        losses = top + jnp.log(total) - label_logit
        probs = jnp.exp(logits - top[:, None]) / total[:, None]
        residue = (probs - target.astype(jnp.float32)).astype(jnp.bfloat16)
        partial_grad = jnp.dot(white_t, residue, preferred_element_type=jnp.float32)
        return (losses, partial_grad)

    losses_first, partial_first = forward(weights)
    block = WHITE // lax.axis_size("dp")
    row_start = lax.axis_index("dp") * block
    grad_whole = lax.psum(partial_first.astype(jnp.bfloat16), "dp").astype(jnp.float32)
    updated = (weights.astype(jnp.float32) - step_size * grad_whole).astype(jnp.bfloat16)
    grad_rows = lax.dynamic_slice_in_dim(grad_whole, row_start, block, 0)
    losses_second, partial_second = forward(updated)
    grad_rows = grad_rows + lax.psum_scatter(
        partial_second.astype(jnp.bfloat16), "dp", scatter_dimension=0, tiled=True
    ).astype(jnp.float32)
    return (jnp.stack([losses_first, losses_second]), grad_rows)


def solution(mesh):
    in_specs = (P(("dp", "cls"), None), P("cls", None), P(None, "cls"), P("dp"))
    out_specs = (P(None, "dp"), P("dp", "cls"))
    return jax.shard_map(shards, mesh=mesh, in_specs=in_specs, out_specs=out_specs, check_vma=False)
```

profile of v0, /device:TPU:1, one launch (start us, length us, event | category | flops | bytes accessed | tf_op | source)
XLA Modules:
  0.0 823.3 jit_solution(9680438581646975648)
XLA Ops:
  7.2 0.0 copy-start
  7.2 0.0 all-gather.3.cloned.1.call-start
  7.2 0.7 all-gather.3.cloned.1.call-update
  7.9 0.0 copy-start.5
  7.9 0.0 all-gather.5.cloned.1.call-start
  8.0 95.6 %all-gather.3.cloned.1.call-done = bf16[512,6144]{1,0:T(8,128)(2,1)} async-done(((bf16[8,6144]{1,0:T(8,128)(2,1)}), bf16[512,6144]{1,0:T(8,128)(2,1)}) %all-gather.3.cloned.1.call-update) | async-done | bytes 6291472 | tf_op jit(solution)/shard_map/all_gather | solution.py:15
  103.6 0.0 copy-done
  103.6 5.4 convolution_convert_fusion.2
  109.0 0.0 all-gather.5.cloned.1.call-update
  109.0 0.0 all-reduce.3.cloned.1.call-start
  109.1 0.0 copy-start.2
  109.1 79.4 %all-gather.5.cloned.1.call-done = bf16[2048,512]{1,0:T(8,128)(2,1)} async-done(((bf16[32,512]{1,0:T(8,128)(2,1)}), bf16[2048,512]{1,0:T(8,128)(2,1)}) %all-gather.5.cloned.1.call-update) | async-done | bytes 2097168 | tf_op jit(solution)/shard_map/all_gather | solution.py:19
  188.5 0.0 copy-done.5
  188.5 2.4 fusion.22
  190.9 123.6 %pmax.14 = f32[512]{0:T(512)S(1)} all-reduce(f32[512]{0:T(512)S(1)} %get-tuple-element.9), channel_id=1, replica_groups=mesh['dp'=8,'cls'=64] {'cls'}, use_global_device_ids=true, to_apply=%region_1.2 | all-reduce | flops 512 | bytes 4096 | tf_op jit(solution)/shard_map/pmax | solution.py:31
  314.5 0.0 copy-done.2
  314.5 0.1 fusion.6
  314.7 126.6 %psum.35 = f32[512]{0:T(512)S(1)} all-reduce(f32[512]{0:T(512)S(1)} %get-tuple-element.3), channel_id=1, replica_groups=mesh['dp'=8,'cls'=64] {'cls'}, use_global_device_ids=true, to_apply=%region_3.4 | all-reduce | flops 512 | bytes 4096 | tf_op jit(solution)/shard_map/psum | solution.py:33
  441.3 3.4 convolution_convert_fusion.1
  444.6 0.0 all-reduce.3.cloned.1.call-update
  444.7 0.0 reduce-scatter.2.cloned.1.call-start
  444.7 76.3 %all-reduce.3.cloned.1.call-done = bf16[2048,256]{1,0:T(8,128)(2,1)} async-done(((bf16[2048,256]{1,0:T(8,128)(2,1)}), bf16[2048,256]{1,0:T(8,128)(2,1)}) %all-reduce.3.cloned.1.call-update) | async-done | bytes 1048592 | tf_op jit(solution)/shard_map/psum | solution.py:43
  521.0 2.6 fusion.23
  523.6 127.9 %pmax.15 = f32[512]{0:T(512)S(1)} all-reduce(f32[512]{0:T(512)S(1)} %get-tuple-element.11), channel_id=1, replica_groups=mesh['dp'=8,'cls'=64] {'cls'}, use_global_device_ids=true, to_apply=%region_8.9 | all-reduce | flops 512 | bytes 4096 | tf_op jit(solution)/shard_map/pmax | solution.py:31
  651.5 0.1 fusion.10
  651.7 127.2 %all-reduce = (f32[512]{0:T(512)S(1)}, f32[512]{0:T(512)S(1)}, f32[512]{0:T(512)}) all-reduce(f32[512]{0:T(512)S(1)} %get-tuple-element.5, f32[512]{0:T(512)S(1)} %get-tuple-element.4, f32[512]{0:T(512)S(1)} %get-tuple-element.2), channel_id=1, replica_groups=mesh['dp'=8,'cls'=64] {'cls'}, use_global_device_ids=true, to_apply=%region_12.13 | all-reduce | flops 1536 | bytes 12288 | tf_op jit(solution)/shard_map/psum | solution.py:33
  778.9 0.0 copy-start.3
  778.9 0.0 copy-start.1
  778.9 3.5 convolution_convert_fusion
  782.3 0.0 reduce-scatter.2.cloned.1.call-update
  782.4 0.0 copy-done.3
  782.4 0.0 copy-done.1
  782.4 0.0 copy-start.4
  782.4 0.2 convert_element_type.36
  782.6 0.5 copy-done.4
  783.1 0.7 add_subtract_fusion
  783.8 0.6 pad_maximum_fusion
  784.4 30.8 %reduce-scatter.2.cloned.1.call-done = bf16[256,256]{1,0:T(8,128)(2,1)} async-done(((bf16[2048,256]{1,0:T(8,128)(2,1)}), bf16[256,256]{1,0:T(8,128)(2,1)}) %reduce-scatter.2.cloned.1.call-update) | async-done | bytes 131088 | tf_op jit(solution)/shard_map/reduce_scatter | solution.py:47
  815.1 1.6 convert_add_fusion
  (1 shorter events, 0.0 us)
Async XLA Ops:
  7.2 96.4 %copy-start = (bf16[32,6144]{1,0:T(8,128)(2,1)S(1)}, bf16[32,6144]{1,0:T(8,128)(2,1)}, u32[]{:S(2)}) copy-start(bf16[32,6144]{1,0:T(8,128)(2,1)} %param.5) | copy-start | bytes 1179652
  7.2 96.4 %all-gather.3.cloned.1.call-start = ((), (), s32[]{:S(2)}) async-start(), calls=%async_computation.1 | async-start | bytes 6389760 | tf_op jit(solution)/shard_map/all_gather | solution.py:15
  7.9 180.6 %copy-start.5 = (bf16[2048,256]{1,0:T(8,128)(2,1)S(1)}, bf16[2048,256]{1,0:T(8,128)(2,1)}, u32[]{:S(2)}) copy-start(bf16[2048,256]{1,0:T(8,128)(2,1)} %param.6) | copy-start | bytes 3145732
  7.9 180.6 %all-gather.5.cloned.1.call-start = ((), (), s32[]{:S(2)}) async-start(), calls=%async_computation.2 | async-start | bytes 2129920 | tf_op jit(solution)/shard_map/all_gather | solution.py:19
  109.0 412.0 %all-reduce.3.cloned.1.call-start = ((), (), s32[]{:S(2)}) async-start(), calls=%async_computation.3 | async-start | bytes 2097152 | tf_op jit(solution)/shard_map/psum | solution.py:43
  109.1 205.5 %copy-start.2 = (s32[512]{0:T(512)S(1)}, s32[512]{0:T(512)}, u32[]{:S(2)}) copy-start(s32[512]{0:T(512)} %param.7) | copy-start | bytes 6148
  444.7 370.5 %reduce-scatter.2.cloned.1.call-start = ((), (), s32[]{:S(2)}) async-start(), calls=%async_computation.4 | async-start | bytes 1179648 | tf_op jit(solution)/shard_map/reduce_scatter | solution.py:47
  778.9 3.5 copy-start.3
  778.9 3.5 copy-start.1
  782.4 0.7 copy-start.4
Sparse Core Ops, SparseCore 0:
  11.4 92.1 all-gather.2
  109.1 79.3 all-gather.4
  444.8 76.1 all-reduce.2
  782.5 32.6 reduce-scatter.1
where the time goes:
time: 827 us; the launch traced here: 823 us
  blocking collectives  505 us (61%)
  waiting for transfers between devices  283 us (34%)
  matrix products  17.3 us (2%)
  between operations  13.9 us (2%)
    psum x2, blocking collectives, forward(): total, label_logit = lax.psum((local_total, picked), 'cls')  254 us
    pmax x2, blocking collectives, forward(): top = lax.pmax(local_top, 'cls')  252 us
    all_gather x1, waiting for transfers between devices, shards(): lax.all_gather(features, 'cls', axis=0, tiled=True)  95.6 us
    all_gather x1, waiting for transfers between devices, shards(): white_t = lax.all_gather(own_rows_white, 'cls', axis=0, tiled=True)  79.4 us
    psum x1, waiting for transfers between devices, shards(): lax.psum(partial_first.astype(jnp.bfloat16), 'dp').astype(jnp.float32)  76.3 us
    reduce_scatter x1, waiting for transfers between devices, shards(): lax.psum_scatter(partial_second.astype(jnp.bfloat16), 'dp', scatter_dimen...  30.8 us
  transfers between devices with their start and end apart: 4, of which 4 were waited for; matrix products, arithmetic and copies ran while one was open for 0% of the time, Pallas kernels for 0%

commit v1 on v0

v1 whole, which is shorter than its diff:
```python
import jax
import jax.numpy as jnp
from jax import lax
from jax.sharding import Mesh
from jax.sharding import PartitionSpec as P

FEAT = 6144
WHITE = 2048
STEP_SCALE = 2.0
Z, Y, X, C = 8, 8, 4, 2
CLS = ("y", "x", "c")


def spread(block, axis, count):
    copies = jnp.broadcast_to(block[None], (count,) + block.shape)
    return lax.all_to_all(copies, axis, 0, 0, tiled=True)


def shards(features, basis, weights, labels):
    basis_rows = lax.all_gather(basis, "x", axis=0, tiled=True)
    image_rows = spread(spread(features, "y", Y), "c", C).reshape(C * Y * 8, FEAT)
    block = lax.dot_general(
        basis_rows, image_rows, (((1,), (1,)), ((), ())), preferred_element_type=jnp.float32
    ).astype(jnp.bfloat16)
    blocks = spread(spread(spread(block, "y", Y), "x", X), "c", C)
    blocks = blocks.reshape(C, X, Y, 4, 32, 128)
    white_t = blocks.transpose(2, 3, 0, 4, 1, 5).reshape(WHITE, 512)
    labels = labels.reshape(Y, X, C, 8).transpose(1, 2, 0, 3).reshape(512)

    width = weights.shape[1]
    class_ids = lax.axis_index(CLS) * width + lax.iota(jnp.int32, width)
    target = class_ids[:, None] == labels[None, :]
    step_size = STEP_SCALE / WHITE

    def forward(current):
        logits = lax.dot_general(
            current, white_t, (((0,), (0,)), ((), ())), preferred_element_type=jnp.float32
        )
        picked = jnp.sum(jnp.where(target, logits, 0.0), axis=0)
        own_top = jnp.max(logits, axis=0)
        own_lse = own_top + jnp.log(jnp.sum(jnp.exp(logits - own_top[None]), axis=0))
        parts = spread(jnp.stack([own_lse, picked]), CLS, Y * X * C)
        lses = parts[:, 0]
        top = jnp.max(lses, axis=0)
        lse = top + jnp.log(jnp.sum(jnp.exp(lses - top[None]), axis=0))
        losses = lse - jnp.sum(parts[:, 1], axis=0)
        residue = (jnp.exp(logits - lse[None]) - target.astype(jnp.float32)).astype(jnp.bfloat16)
        partial = lax.dot_general(
            white_t, residue, (((1,), (1,)), ((), ())), preferred_element_type=jnp.float32
        ).astype(jnp.bfloat16)
        pieces = lax.all_to_all(partial.reshape(Z, WHITE // Z, width), "z", 0, 0, tiled=True)
        return losses, jnp.sum(pieces.astype(jnp.float32), axis=0)

    losses_first, grad_first = forward(weights)
    own_rows = lax.dynamic_slice_in_dim(weights, lax.axis_index("z") * (WHITE // Z), WHITE // Z, 0)
    own_updated = (own_rows.astype(jnp.float32) - step_size * grad_first).astype(jnp.bfloat16)
    updated = spread(own_updated, "z", Z).reshape(WHITE, width)
    losses_second, grad_second = forward(updated)
    losses = jnp.stack([losses_first, losses_second])
    losses = losses.reshape(2, X, C, Y, 8).transpose(0, 3, 1, 2, 4).reshape(2, 512)
    return losses, grad_first + grad_second


def solution(mesh):
    fine = Mesh(mesh.devices.reshape(Z, Y, X, C), ("z", "y", "x", "c"))
    in_specs = (P(("z",) + CLS, None), P(CLS, None), P(None, CLS), P("z"))
    out_specs = (P(None, "z"), P("z", CLS))
    return jax.shard_map(shards, mesh=fine, in_specs=in_specs, out_specs=out_specs, check_vma=False)
```

time: 827 us -> 247 us (0.30)
  blocking collectives: 505 us -> 128 us
  waiting for transfers between devices: 283 us -> 72.5 us
  starting transfers between devices: 0.16 us -> 14.2 us
  matrix products: 17.3 us -> 7.16 us
    psum x2 -> x0, blocking collectives: 254 us -> none  [forward(): total, label_logit = lax.psum((local_total, picked), 'cls')]
    pmax x2 -> x0, blocking collectives: 252 us -> none  [forward(): top = lax.pmax(local_top, 'cls')]
    all_gather x2 -> x1, waiting for transfers between devices: 175 us -> 2.31 us  [shards(): basis_rows = lax.all_gather(basis, 'x', axis=0, tiled=True)]
    all_to_all x0 -> x7, blocking collectives: none -> 128 us  [spread(): return lax.all_to_all(copies, axis, 0, 0, tiled=True)]
    psum x1 -> x0, waiting for transfers between devices: 76.3 us -> none  [shards(): lax.psum(partial_first.astype(jnp.bfloat16), 'dp').astype(jnp.float32)]
    all_to_all x0 -> x3, waiting for transfers between devices: none -> 69.5 us  [the longest x2 57.4 us: forward(): lax.all_to_all(partial.reshape(Z, WHITE // Z, width), 'z', 0, 0, tiled=True)]
    reduce_scatter x1 -> x0, waiting for transfers between devices: 30.8 us -> none  [shards(): lax.psum_scatter(partial_second.astype(jnp.bfloat16), 'dp', scatter_dimen...]
    all_to_all x0 -> x3, starting transfers between devices: none -> 14.2 us  [the longest x2 10.7 us: forward(): lax.all_to_all(partial.reshape(Z, WHITE // Z, width), 'z', 0, 0, tiled=True)]
  transfers between devices with their start and end apart: 4 -> 4, of which waited for: 4 -> 4; matrix products, arithmetic and copies ran while one was open for 0% -> 1% of each run, Pallas kernels for 0% -> 0%
where the time goes in v1:
time: 247 us; the launch traced here: 246 us
  blocking collectives  128 us (52%)
  waiting for transfers between devices  72.5 us (29%)
  between operations  14.3 us (6%)
  starting transfers between devices  14.2 us (6%)
  matrix products  7.16 us (3%)
  local copies, waits for them, and re-layouts  6.94 us (3%)
  other arithmetic  2.97 us (1%)
    all_to_all x7, blocking collectives, spread(): return lax.all_to_all(copies, axis, 0, 0, tiled=True)  128 us
    all_to_all x2, waiting for transfers between devices, forward(): lax.all_to_all(partial.reshape(Z, WHITE // Z, width), 'z', 0, 0, tiled=True)  57.4 us
    all_to_all x1, waiting for transfers between devices, spread(): return lax.all_to_all(copies, axis, 0, 0, tiled=True)  12.1 us
    all_to_all x2, starting transfers between devices, forward(): lax.all_to_all(partial.reshape(Z, WHITE // Z, width), 'z', 0, 0, tiled=True)  10.7 us
  transfers between devices with their start and end apart: 4, of which 4 were waited for; matrix products, arithmetic and copies ran while one was open for 1% of the time, Pallas kernels for 0%

profile of v1, /device:TPU:1, one launch (start us, length us, event | category | flops | bytes accessed | tf_op | source)
XLA Modules:
  0.0 246.3 jit_solution(5977529367981085806)
XLA Ops:
  7.2 0.0 all-gather.2.cloned.1.call-start
  7.2 0.7 all-gather.2.cloned.1.call-update
  7.9 0.9 broadcast_in_dim.20
  8.8 27.8 %all_to_all.50 = bf16[8,8,6144]{2,1,0:T(8,128)(2,1)S(1)} all-to-all(bf16[8,8,6144]{2,1,0:T(8,128)(2,1)S(1)} %broadcast_in_dim.20), channel_id=1, replica_groups=mesh['z'=8,'y'=8,'x'=4,'c'=2] {'y'}, dimensions={0} | all-to-all | bytes 1572864 | tf_op jit(solution)/shard_map/all_to_all | solution.py:16
  36.6 0.2 broadcast_in_dim.21
  36.8 8.3 %all_to_all.51 = bf16[2,8,8,6144]{3,2,1,0:T(8,128)(2,1)S(1)} all-to-all(bf16[2,8,8,6144]{3,2,1,0:T(8,128)(2,1)S(1)} %broadcast_in_dim.21), channel_id=1, replica_groups=mesh['z'=8,'y'=8,'x'=4,'c'=2] {'c'}, dimensions={0} | all-to-all | bytes 3145728 | tf_op jit(solution)/shard_map/all_to_all | solution.py:16
  45.2 2.3 all-gather.2.cloned.1.call-done
  47.5 2.0 convolution_convert_fusion.2
  49.5 0.0 copy-start.1
  49.5 16.6 %all_to_all.52 = bf16[8,128,128]{2,1,0:T(8,128)(2,1)S(1)} all-to-all(bf16[8,128,128]{2,1,0:T(8,128)(2,1)S(1)} %broadcast_in_dim.23), channel_id=1, replica_groups=mesh['z'=8,'y'=8,'x'=4,'c'=2] {'y'}, dimensions={0} | all-to-all | bytes 524288 | tf_op jit(solution)/shard_map/all_to_all | solution.py:16
  66.2 1.2 broadcast_in_dim.24
  67.4 3.5 %all-to-all-start.3 = ((bf16[4,8,128,128]{3,2,1,0:T(8,128)(2,1)}), bf16[4,8,128,128]{3,2,1,0:T(8,128)(2,1)S(1)}, u32[]{:S(2)}, u32[]{:S(2)}) async-start(bf16[4,8,128,128]{3,2,1,0:T(8,128)(2,1)} %broadcast_in_dim.24), calls=%async_computation.3 | async-start | bytes 2097152 | tf_op jit(solution)/shard_map/all_to_all | solution.py:16
  70.9 0.0 copy-done.1
  70.9 0.1 reshape.167
  71.1 0.1 eq.16
  71.2 12.1 %all-to-all-done.3 = bf16[4,8,128,128]{3,2,1,0:T(8,128)(2,1)S(1)} async-done(((bf16[4,8,128,128]{3,2,1,0:T(8,128)(2,1)}), bf16[4,8,128,128]{3,2,1,0:T(8,128)(2,1)S(1)}, u32[]{:S(2)}, u32[]{:S(2)}) %all-to-all-start.3) | async-done | bytes 1048608 | tf_op jit(solution)/shard_map/all_to_all | solution.py:16
  83.3 0.5 broadcast_in_dim.25
  83.8 8.7 %all_to_all.53 = bf16[2,4,8,128,128]{4,3,2,1,0:T(8,128)(2,1)S(1)} all-to-all(bf16[2,4,8,128,128]{4,3,2,1,0:T(8,128)(2,1)S(1)} %broadcast_in_dim.25), channel_id=1, replica_groups=mesh['z'=8,'y'=8,'x'=4,'c'=2] {'c'}, dimensions={0} | all-to-all | bytes 4194304 | tf_op jit(solution)/shard_map/all_to_all | solution.py:16
  92.5 0.0 copy-start
  92.5 2.7 %copy.12 = bf16[8,4,2,32,4,128]{5,4,3,2,1,0:T(4,128)(2,1)S(1)} copy(bf16[8,4,2,32,4,128]{5,3,1,0,4,2:T(8,128)(2,1)S(1)} %bitcast.60) | data formatting | bytes 4194304 | tf_op jit(solution)/shard_map/transpose | solution.py:27
  95.2 0.0 copy-done
  95.2 0.8 fusion.33
  96.0 0.1 fusion.17
  96.2 0.1 broadcast_in_dim.27
  96.2 17.5 %all_to_all.54 = f32[64,2,512]{2,1,0:T(2,128)S(1)} all-to-all(f32[64,2,512]{2,1,0:T(2,128)S(1)} %broadcast_in_dim.27), channel_id=1, replica_groups=mesh['z'=8,'y'=8,'x'=4,'c'=2] {'y','x','c'}, dimensions={0} | all-to-all | bytes 524288 | tf_op jit(solution)/shard_map/all_to_all | solution.py:16
  113.8 0.3 slice_reduce_fusion.1
  114.1 1.8 convolution_convert_fusion.1
  115.9 7.1 %all-to-all-start.6 = ((bf16[8,256,256]{2,1,0:T(8,128)(2,1)}), bf16[8,256,256]{2,1,0:T(8,128)(2,1)S(1)}, u32[]{:S(2)}, u32[]{:S(2)}) async-start(bf16[8,256,256]{2,1,0:T(8,128)(2,1)} %bitcast.66), calls=%async_computation.6 | async-start | bytes 2097152 | tf_op jit(solution)/shard_map/all_to_all | solution.py:51
  123.0 29.2 %all-to-all-done.6 = bf16[8,256,256]{2,1,0:T(8,128)(2,1)S(1)} async-done(((bf16[8,256,256]{2,1,0:T(8,128)(2,1)}), bf16[8,256,256]{2,1,0:T(8,128)(2,1)S(1)}, u32[]{:S(2)}, u32[]{:S(2)}) %all-to-all-start.6) | async-done | bytes 1048608 | tf_op jit(solution)/shard_map/all_to_all | solution.py:51
  152.3 0.1 convert_reduce_fusion.1
  152.4 1.0 subtract_convert_fusion
  153.4 0.1 broadcast_in_dim.28
  153.4 31.4 %all_to_all.55 = bf16[8,256,256]{2,1,0:T(8,128)(2,1)S(1)} all-to-all(bf16[8,256,256]{2,1,0:T(8,128)(2,1)S(1)} %broadcast_in_dim.28), channel_id=1, replica_groups=mesh['z'=8,'y'=8,'x'=4,'c'=2] {'z'}, dimensions={0} | all-to-all | bytes 2097152 | tf_op jit(solution)/shard_map/all_to_all | solution.py:16
  184.8 0.7 fusion.34
  185.6 0.1 exponential_reduce_fusion
  185.7 0.1 broadcast_in_dim.29
  185.8 17.9 %all_to_all.56 = f32[64,2,512]{2,1,0:T(2,128)S(1)} all-to-all(f32[64,2,512]{2,1,0:T(2,128)S(1)} %broadcast_in_dim.29), channel_id=1, replica_groups=mesh['z'=8,'y'=8,'x'=4,'c'=2] {'y','x','c'}, dimensions={0} | all-to-all | bytes 524288 | tf_op jit(solution)/shard_map/all_to_all | solution.py:16
  203.7 0.3 slice_reduce_fusion
  204.0 1.8 convolution_convert_fusion
  205.8 3.6 %all-to-all-start.9 = ((bf16[8,256,256]{2,1,0:T(8,128)(2,1)}), bf16[8,256,256]{2,1,0:T(8,128)(2,1)S(1)}, u32[]{:S(2)}, u32[]{:S(2)}) async-start(bf16[8,256,256]{2,1,0:T(8,128)(2,1)} %bitcast.12), calls=%async_computation.9 | async-start | bytes 2097152 | tf_op jit(solution)/shard_map/all_to_all | solution.py:51
  209.4 0.1 sub.90
  209.5 0.1 sub.100
  209.6 0.7 reshape.170
  210.4 28.2 %all-to-all-done.9 = bf16[8,256,256]{2,1,0:T(8,128)(2,1)S(1)} async-done(((bf16[8,256,256]{2,1,0:T(8,128)(2,1)}), bf16[8,256,256]{2,1,0:T(8,128)(2,1)S(1)}, u32[]{:S(2)}, u32[]{:S(2)}) %all-to-all-start.9) | async-done | bytes 1048608 | tf_op jit(solution)/shard_map/all_to_all | solution.py:51
  238.6 0.1 convert_reduce_fusion
  238.7 0.7 add.91
  (13 shorter events, 0.2 us)
Async XLA Ops:
  7.2 40.3 %all-gather.2.cloned.1.call-start = ((), (), s32[]{:S(2)}) async-start(), calls=%async_computation.10 | async-start | bytes 1966080 | tf_op jit(solution)/shard_map/all_gather | solution.py:20
  49.5 21.4 %copy-start.1 = (s32[512]{0:T(512)S(1)}, s32[512]{0:T(512)}, u32[]{:S(2)}) copy-start(s32[512]{0:T(512)} %param.7) | copy-start | bytes 6148
  67.4 15.9 %all-to-all-start.3 = ((bf16[4,8,128,128]{3,2,1,0:T(8,128)(2,1)}), bf16[4,8,128,128]{3,2,1,0:T(8,128)(2,1)S(1)}, u32[]{:S(2)}, u32[]{:S(2)}) async-start(bf16[4,8,128,128]{3,2,1,0:T(8,128)(2,1)} %broadcast_in_dim.24), calls=%async_computation.3 | async-start | bytes 2097152 | tf_op jit(solution)/shard_map/all_to_all | solution.py:16
  92.5 2.7 %copy-start = (bf16[2048,256]{1,0:T(8,128)(2,1)S(1)}, bf16[2048,256]{1,0:T(8,128)(2,1)}, u32[]{:S(2)}) copy-start(bf16[2048,256]{1,0:T(8,128)(2,1)} %param.6) | copy-start | bytes 3145732
  115.9 36.3 %all-to-all-start.6 = ((bf16[8,256,256]{2,1,0:T(8,128)(2,1)}), bf16[8,256,256]{2,1,0:T(8,128)(2,1)S(1)}, u32[]{:S(2)}, u32[]{:S(2)}) async-start(bf16[8,256,256]{2,1,0:T(8,128)(2,1)} %bitcast.66), calls=%async_computation.6 | async-start | bytes 2097152 | tf_op jit(solution)/shard_map/all_to_all | solution.py:51
  205.8 32.7 %all-to-all-start.9 = ((bf16[8,256,256]{2,1,0:T(8,128)(2,1)}), bf16[8,256,256]{2,1,0:T(8,128)(2,1)S(1)}, u32[]{:S(2)}, u32[]{:S(2)}) async-start(bf16[8,256,256]{2,1,0:T(8,128)(2,1)} %bitcast.12), calls=%async_computation.9 | async-start | bytes 2097152 | tf_op jit(solution)/shard_map/all_to_all | solution.py:51
Sparse Core Ops, SparseCore 0:
  10.1 37.3 all-gather.1

commit v2 on v1

--- a/solution.py
+++ b/solution.py
@@ -16,12 +16,32 @@
     return lax.all_to_all(copies, axis, 0, 0, tiled=True)
 
 
+def ring(block, axis, count):
+    back = [[(at, (at - away) % count) for at in range(count)] for away in range(1, count)]
+    return [block] + [lax.ppermute(block, axis, pairs) for pairs in back]
+
+
+def in_order(rolled, axis, count):
+    twice = jnp.concatenate([rolled, rolled])
+    rows = rolled.shape[0]
+    first = (count - lax.axis_index(axis)) * (rows // count)
+    return lax.dynamic_slice_in_dim(twice, first, rows, 0)
+
+
+def joined(parts):
+    top = jnp.max(parts[:, 0], axis=0)
+    total = jnp.sum(parts[:, 1] * jnp.exp(parts[:, 0] - top[None]), axis=0)
+    return top, total, jnp.sum(parts[:, 2], axis=0)
+
+
 def shards(features, basis, weights, labels):
-    basis_rows = lax.all_gather(basis, "x", axis=0, tiled=True)
+    basis_rows = ring(basis, "x", X)
     image_rows = spread(spread(features, "y", Y), "c", C).reshape(C * Y * 8, FEAT)
-    block = lax.dot_general(
-        basis_rows, image_rows, (((1,), (1,)), ((), ())), preferred_element_type=jnp.float32
-    ).astype(jnp.bfloat16)
+    rolled = jnp.concatenate([
+        lax.dot_general(rows, image_rows, (((1,), (1,)), ((), ())), preferred_element_type=jnp.float32)
+        for rows in basis_rows
+    ])
+    block = in_order(rolled.astype(jnp.bfloat16), "x", X)
     blocks = spread(spread(spread(block, "y", Y), "x", X), "c", C)
     blocks = blocks.reshape(C, X, Y, 4, 32, 128)
     white_t = blocks.transpose(2, 3, 0, 4, 1, 5).reshape(WHITE, 512)
@@ -38,13 +58,16 @@
         )
         picked = jnp.sum(jnp.where(target, logits, 0.0), axis=0)
         own_top = jnp.max(logits, axis=0)
-        own_lse = own_top + jnp.log(jnp.sum(jnp.exp(logits - own_top[None]), axis=0))
-        parts = spread(jnp.stack([own_lse, picked]), CLS, Y * X * C)
-        lses = parts[:, 0]
-        top = jnp.max(lses, axis=0)
-        lse = top + jnp.log(jnp.sum(jnp.exp(lses - top[None]), axis=0))
-        losses = lse - jnp.sum(parts[:, 1], axis=0)
-        residue = (jnp.exp(logits - lse[None]) - target.astype(jnp.float32)).astype(jnp.bfloat16)
+        own_total = jnp.sum(jnp.exp(logits - own_top[None]), axis=0)
+        own = jnp.stack([own_top, own_total, picked])
+        other = lax.ppermute(own, "c", [(0, 1), (1, 0)])
+        first = lax.axis_index("c") == 0
+        pair = joined(jnp.stack([jnp.where(first, own, other), jnp.where(first, other, own)]))
+        parts = spread(jnp.stack(pair).reshape(12, 128), ("y", "x"), Y * X)
+        top, total, label_logit = joined(parts.reshape(Y * X, 3, 512))
+        losses = top + jnp.log(total) - label_logit
+        probs = jnp.exp(logits - top[None]) / total[None]
+        residue = (probs - target.astype(jnp.float32)).astype(jnp.bfloat16)
         partial = lax.dot_general(
             white_t, residue, (((1,), (1,)), ((), ())), preferred_element_type=jnp.float32
         ).astype(jnp.bfloat16)

time: 247 us -> 236 us (0.955)
  blocking collectives: 128 us -> 89.5 us
  starting transfers between devices: 14.2 us -> 41.1 us
  between operations: 14.3 us -> 1.02 us
  waiting for transfers between devices: 72.5 us -> 84.6 us
    all_to_all x7 -> x6, blocking collectives: 128 us -> 89.5 us  [spread(): return lax.all_to_all(copies, axis, 0, 0, tiled=True)]
    ppermute x0 -> x5, starting transfers between devices: none -> 14.7 us  [the longest x3 9.33 us: ring(): return [block] + [lax.ppermute(block, axis, pairs) for pairs in back]]
    all_to_all x1 -> x2, waiting for transfers between devices: 12.1 us -> 25.8 us  [spread(): return lax.all_to_all(copies, axis, 0, 0, tiled=True)]
    all_to_all x1 -> x2, starting transfers between devices: 3.51 us -> 12.8 us  [spread(): return lax.all_to_all(copies, axis, 0, 0, tiled=True)]
    all_to_all x2, starting transfers between devices: 10.7 us -> 13.6 us  [forward(): lax.all_to_all(partial.reshape(Z, WHITE // Z, width), 'z', 0, 0, tiled=True)]
  transfers between devices with their start and end apart: 4 -> 9, of which waited for: 4 -> 6; matrix products, arithmetic and copies ran while one was open for 1% -> 1% of each run, Pallas kernels for 0% -> 0%
where the time goes in v2:
time: 236 us; the launch traced here: 235 us
  blocking collectives  89.5 us (38%)
  waiting for transfers between devices  84.6 us (36%)
  starting transfers between devices  41.1 us (17%)
  local copies, waits for them, and re-layouts  7.99 us (3%)
  matrix products  7.72 us (3%)
  other arithmetic  2.93 us (1%)
    all_to_all x6, blocking collectives, spread(): return lax.all_to_all(copies, axis, 0, 0, tiled=True)  89.5 us
    all_to_all x2, waiting for transfers between devices, forward(): lax.all_to_all(partial.reshape(Z, WHITE // Z, width), 'z', 0, 0, tiled=True)  57.1 us
    all_to_all x2, waiting for transfers between devices, spread(): return lax.all_to_all(copies, axis, 0, 0, tiled=True)  25.8 us
    all_to_all x2, starting transfers between devices, forward(): lax.all_to_all(partial.reshape(Z, WHITE // Z, width), 'z', 0, 0, tiled=True)  13.6 us
    all_to_all x2, starting transfers between devices, spread(): return lax.all_to_all(copies, axis, 0, 0, tiled=True)  12.8 us
    ppermute x3, starting transfers between devices, ring(): return [block] + [lax.ppermute(block, axis, pairs) for pairs in back]  9.33 us
    ppermute x2, starting transfers between devices, forward(): other = lax.ppermute(own, 'c', [(0, 1), (1, 0)])  5.36 us
  transfers between devices with their start and end apart: 9, of which 6 were waited for; matrix products, arithmetic and copies ran while one was open for 1% of the time, Pallas kernels for 0%

profile of v2, /device:TPU:1, one launch (start us, length us, event | category | flops | bytes accessed | tf_op | source)
XLA Modules:
  0.0 234.8 jit_solution(6320186212881072444)
XLA Ops:
  0.6 1.9 broadcast_in_dim.25
  2.5 7.7 %all-to-all-start = ((bf16[8,8,6144]{2,1,0:T(8,128)(2,1)}), bf16[8,8,6144]{2,1,0:T(8,128)(2,1)S(1)}, u32[]{:S(2)}, u32[]{:S(2)}) async-start(bf16[8,8,6144]{2,1,0:T(8,128)(2,1)} %broadcast_in_dim.25), calls=%async_computation | async-start | bytes 1572864 | tf_op jit(solution)/shard_map/all_to_all | solution.py:16
  10.2 4.4 %collective-permute-start = (bf16[32,6144]{1,0:T(8,128)(2,1)S(1)}, bf16[32,6144]{1,0:T(8,128)(2,1)S(1)}, u32[]{:S(2)}, u32[]{:S(2)}) collective-permute-start(bf16[32,6144]{1,0:T(8,128)(2,1)S(1)} %copy-done), channel_id=1, source_target_pairs={{0,6},{2,0},{4,2},{6,4},{1,7},{3,1},{5,3},{7,5},{8,14},{10,8},{12,... | collective-permute-start | bytes 1179656 | tf_op jit(solution)/shard_map/ppermute | solution.py:21
  14.6 2.4 %collective-permute-start.1 = (bf16[32,6144]{1,0:T(8,128)(2,1)S(1)}, bf16[32,6144]{1,0:T(8,128)(2,1)S(1)}, u32[]{:S(2)}, u32[]{:S(2)}) collective-permute-start(bf16[32,6144]{1,0:T(8,128)(2,1)S(1)} %copy-done), channel_id=1, source_target_pairs={{0,4},{2,6},{4,0},{6,2},{1,5},{3,7},{5,1},{7,3},{8,12},{10,14},{12... | collective-permute-start | bytes 1179656 | tf_op jit(solution)/shard_map/ppermute | solution.py:21
  17.0 2.5 %collective-permute-start.2 = (bf16[32,6144]{1,0:T(8,128)(2,1)S(1)}, bf16[32,6144]{1,0:T(8,128)(2,1)S(1)}, u32[]{:S(2)}, u32[]{:S(2)}) collective-permute-start(bf16[32,6144]{1,0:T(8,128)(2,1)S(1)} %copy-done), channel_id=1, source_target_pairs={{0,2},{2,4},{4,6},{6,0},{1,3},{3,5},{5,7},{7,1},{8,10},{10,12},{12... | collective-permute-start | bytes 1179656 | tf_op jit(solution)/shard_map/ppermute | solution.py:21
  19.5 11.7 %all-to-all-done = bf16[8,8,6144]{2,1,0:T(8,128)(2,1)S(1)} async-done(((bf16[8,8,6144]{2,1,0:T(8,128)(2,1)}), bf16[8,8,6144]{2,1,0:T(8,128)(2,1)S(1)}, u32[]{:S(2)}, u32[]{:S(2)}) %all-to-all-start) | async-done | bytes 786464 | tf_op jit(solution)/shard_map/all_to_all | solution.py:16
  31.2 0.1 broadcast_in_dim.26
  31.3 7.7 %all_to_all.50 = bf16[2,8,8,6144]{3,2,1,0:T(8,128)(2,1)S(1)} all-to-all(bf16[2,8,8,6144]{3,2,1,0:T(8,128)(2,1)S(1)} %broadcast_in_dim.26), channel_id=1, replica_groups=mesh['z'=8,'y'=8,'x'=4,'c'=2] {'c'}, dimensions={0} | all-to-all | bytes 3145728 | tf_op jit(solution)/shard_map/all_to_all | solution.py:16
  39.1 0.6 constant_dynamic-update-slice_fusion.7
  39.7 0.6 constant_dynamic-update-slice_fusion.6
  40.4 0.6 constant_dynamic-update-slice_fusion.5
  41.0 0.6 constant_dynamic-update-slice_fusion.4
  41.8 13.5 %all_to_all.51 = bf16[8,128,128]{2,1,0:T(8,128)(2,1)S(1)} all-to-all(bf16[8,128,128]{2,1,0:T(8,128)(2,1)S(1)} %broadcast_in_dim.27), channel_id=1, replica_groups=mesh['z'=8,'y'=8,'x'=4,'c'=2] {'y'}, dimensions={0} | all-to-all | bytes 524288 | tf_op jit(solution)/shard_map/all_to_all | solution.py:16
  55.3 1.2 broadcast_in_dim.28
  56.6 5.2 %all-to-all-start.3 = ((bf16[4,8,128,128]{3,2,1,0:T(8,128)(2,1)}), bf16[4,8,128,128]{3,2,1,0:T(8,128)(2,1)S(1)}, u32[]{:S(2)}, u32[]{:S(2)}) async-start(bf16[4,8,128,128]{3,2,1,0:T(8,128)(2,1)} %broadcast_in_dim.28), calls=%async_computation.3 | async-start | bytes 2097152 | tf_op jit(solution)/shard_map/all_to_all | solution.py:16
  61.8 0.1 reshape.133
  61.9 0.1 eq.21
  62.0 14.2 %all-to-all-done.3 = bf16[4,8,128,128]{3,2,1,0:T(8,128)(2,1)S(1)} async-done(((bf16[4,8,128,128]{3,2,1,0:T(8,128)(2,1)}), bf16[4,8,128,128]{3,2,1,0:T(8,128)(2,1)S(1)}, u32[]{:S(2)}, u32[]{:S(2)}) %all-to-all-start.3) | async-done | bytes 1048608 | tf_op jit(solution)/shard_map/all_to_all | solution.py:16
  76.2 0.5 broadcast_in_dim.29
  76.7 6.7 %all_to_all.52 = bf16[2,4,8,128,128]{4,3,2,1,0:T(8,128)(2,1)S(1)} all-to-all(bf16[2,4,8,128,128]{4,3,2,1,0:T(8,128)(2,1)S(1)} %broadcast_in_dim.29), channel_id=1, replica_groups=mesh['z'=8,'y'=8,'x'=4,'c'=2] {'c'}, dimensions={0} | all-to-all | bytes 4194304 | tf_op jit(solution)/shard_map/all_to_all | solution.py:16
  83.4 2.7 %copy.21 = bf16[8,4,2,32,4,128]{5,4,3,2,1,0:T(4,128)(2,1)S(1)} copy(bf16[8,4,2,32,4,128]{5,3,1,0,4,2:T(8,128)(2,1)S(1)} %bitcast.122) | data formatting | bytes 4194304 | tf_op jit(solution)/shard_map/transpose | solution.py:47
  86.1 0.8 fusion.52
  86.9 0.1 fusion.17
  87.0 2.3 collective-permute-start.3
  89.3 0.8 collective-permute-done.3
  90.3 14.9 %all_to_all.53 = f32[32,12,128]{2,1,0:T(8,128)S(1)} all-to-all(f32[32,12,128]{2,1,0:T(8,128)S(1)} %broadcast_in_dim.32), channel_id=1, replica_groups=mesh['z'=8,'y'=8,'x'=4,'c'=2] {'y','x'}, dimensions={0} | all-to-all | bytes 393216 | tf_op jit(solution)/shard_map/all_to_all | solution.py:16
  105.1 0.1 reshape.134
  105.2 0.2 slice_reduce_fusion.1
  105.4 1.8 convolution_convert_fusion.1
  107.2 10.0 %all-to-all-start.6 = ((bf16[8,256,256]{2,1,0:T(8,128)(2,1)}), bf16[8,256,256]{2,1,0:T(8,128)(2,1)S(1)}, u32[]{:S(2)}, u32[]{:S(2)}) async-start(bf16[8,256,256]{2,1,0:T(8,128)(2,1)} %bitcast.127), calls=%async_computation.6 | async-start | bytes 2097152 | tf_op jit(solution)/shard_map/all_to_all | solution.py:74
  117.3 29.1 %all-to-all-done.6 = bf16[8,256,256]{2,1,0:T(8,128)(2,1)S(1)} async-done(((bf16[8,256,256]{2,1,0:T(8,128)(2,1)}), bf16[8,256,256]{2,1,0:T(8,128)(2,1)S(1)}, u32[]{:S(2)}, u32[]{:S(2)}) %all-to-all-start.6) | async-done | bytes 1048608 | tf_op jit(solution)/shard_map/all_to_all | solution.py:74
  146.4 0.1 convert_reduce_fusion.1
  146.5 1.0 subtract_convert_fusion
  147.5 30.9 %all_to_all.54 = bf16[8,256,256]{2,1,0:T(8,128)(2,1)S(1)} all-to-all(bf16[8,256,256]{2,1,0:T(8,128)(2,1)S(1)} %broadcast_in_dim.33), channel_id=1, replica_groups=mesh['z'=8,'y'=8,'x'=4,'c'=2] {'z'}, dimensions={0} | all-to-all | bytes 2097152 | tf_op jit(solution)/shard_map/all_to_all | solution.py:16
  178.5 0.8 fusion.53
  179.3 0.1 exponential_reduce_fusion
  179.4 3.1 %collective-permute-start.4 = (f32[3,512]{1,0:T(4,128)S(1)}, f32[3,512]{1,0:T(4,128)S(1)}, u32[]{:S(2)}, u32[]{:S(2)}) collective-permute-start(f32[3,512]{1,0:T(4,128)S(1)} %pad_maximum_fusion.2), channel_id=1, source_target_pairs={{0,1},{1,0},{2,3},{3,2},{4,5},{5,4},{6,7},{7,6},{8,9},{9,8},{10,11... | collective-permute-start | bytes 18440 | tf_op jit(solution)/shard_map/ppermute | solution.py:63
  182.5 0.8 collective-permute-done.4
  183.5 15.7 %all_to_all.55 = f32[32,12,128]{2,1,0:T(8,128)S(1)} all-to-all(f32[32,12,128]{2,1,0:T(8,128)S(1)} %broadcast_in_dim.35), channel_id=1, replica_groups=mesh['z'=8,'y'=8,'x'=4,'c'=2] {'y','x'}, dimensions={0} | all-to-all | bytes 393216 | tf_op jit(solution)/shard_map/all_to_all | solution.py:16
  199.3 0.2 slice_reduce_fusion.2
  199.5 1.8 convolution_convert_fusion
  201.3 3.6 %all-to-all-start.9 = ((bf16[8,256,256]{2,1,0:T(8,128)(2,1)}), bf16[8,256,256]{2,1,0:T(8,128)(2,1)S(1)}, u32[]{:S(2)}, u32[]{:S(2)}) async-start(bf16[8,256,256]{2,1,0:T(8,128)(2,1)} %bitcast.28), calls=%async_computation.9 | async-start | bytes 2097152 | tf_op jit(solution)/shard_map/all_to_all | solution.py:74
  204.9 0.1 sub.112
  205.0 0.1 sub.124
  205.1 0.7 reshape.138
  205.9 28.0 %all-to-all-done.9 = bf16[8,256,256]{2,1,0:T(8,128)(2,1)S(1)} async-done(((bf16[8,256,256]{2,1,0:T(8,128)(2,1)}), bf16[8,256,256]{2,1,0:T(8,128)(2,1)S(1)}, u32[]{:S(2)}, u32[]{:S(2)}) %all-to-all-start.9) | async-done | bytes 1048608 | tf_op jit(solution)/shard_map/all_to_all | solution.py:74
  233.9 0.1 convert_reduce_fusion
  234.1 0.7 add.57
  (41 shorter events, 0.7 us)
Async XLA Ops:
  0.6 9.5 %copy-start = (bf16[32,6144]{1,0:T(8,128)(2,1)S(1)}, bf16[32,6144]{1,0:T(8,128)(2,1)}, u32[]{:S(2)}) copy-start(bf16[32,6144]{1,0:T(8,128)(2,1)} %param.5) | copy-start | bytes 1179652
  2.5 28.7 %all-to-all-start = ((bf16[8,8,6144]{2,1,0:T(8,128)(2,1)}), bf16[8,8,6144]{2,1,0:T(8,128)(2,1)S(1)}, u32[]{:S(2)}, u32[]{:S(2)}) async-start(bf16[8,8,6144]{2,1,0:T(8,128)(2,1)} %broadcast_in_dim.25), calls=%async_computation | async-start | bytes 1572864 | tf_op jit(solution)/shard_map/all_to_all | solution.py:16
  10.2 29.5 %collective-permute-start = (bf16[32,6144]{1,0:T(8,128)(2,1)S(1)}, bf16[32,6144]{1,0:T(8,128)(2,1)S(1)}, u32[]{:S(2)}, u32[]{:S(2)}) collective-permute-start(bf16[32,6144]{1,0:T(8,128)(2,1)S(1)} %copy-done), channel_id=1, source_target_pairs={{0,6},{2,0},{4,2},{6,4},{1,7},{3,1},{5,3},{7,5},{8,14},{10,8},{12,... | collective-permute-start | bytes 1179656 | tf_op jit(solution)/shard_map/ppermute | solution.py:21
  14.6 25.8 %collective-permute-start.1 = (bf16[32,6144]{1,0:T(8,128)(2,1)S(1)}, bf16[32,6144]{1,0:T(8,128)(2,1)S(1)}, u32[]{:S(2)}, u32[]{:S(2)}) collective-permute-start(bf16[32,6144]{1,0:T(8,128)(2,1)S(1)} %copy-done), channel_id=1, source_target_pairs={{0,4},{2,6},{4,0},{6,2},{1,5},{3,7},{5,1},{7,3},{8,12},{10,14},{12... | collective-permute-start | bytes 1179656 | tf_op jit(solution)/shard_map/ppermute | solution.py:21
  17.0 24.0 %collective-permute-start.2 = (bf16[32,6144]{1,0:T(8,128)(2,1)S(1)}, bf16[32,6144]{1,0:T(8,128)(2,1)S(1)}, u32[]{:S(2)}, u32[]{:S(2)}) collective-permute-start(bf16[32,6144]{1,0:T(8,128)(2,1)S(1)} %copy-done), channel_id=1, source_target_pairs={{0,2},{2,4},{4,6},{6,0},{1,3},{3,5},{5,7},{7,1},{8,10},{10,12},{12... | collective-permute-start | bytes 1179656 | tf_op jit(solution)/shard_map/ppermute | solution.py:21
  41.7 20.0 %copy-start.2 = (s32[512]{0:T(512)S(1)}, s32[512]{0:T(512)}, u32[]{:S(2)}) copy-start(s32[512]{0:T(512)} %param.7) | copy-start | bytes 6148
  56.6 19.6 %all-to-all-start.3 = ((bf16[4,8,128,128]{3,2,1,0:T(8,128)(2,1)}), bf16[4,8,128,128]{3,2,1,0:T(8,128)(2,1)S(1)}, u32[]{:S(2)}, u32[]{:S(2)}) async-start(bf16[4,8,128,128]{3,2,1,0:T(8,128)(2,1)} %broadcast_in_dim.28), calls=%async_computation.3 | async-start | bytes 2097152 | tf_op jit(solution)/shard_map/all_to_all | solution.py:16
  83.3 2.7 %copy-start.1 = (bf16[2048,256]{1,0:T(8,128)(2,1)S(1)}, bf16[2048,256]{1,0:T(8,128)(2,1)}, u32[]{:S(2)}) copy-start(bf16[2048,256]{1,0:T(8,128)(2,1)} %param.6) | copy-start | bytes 3145732
  87.0 3.1 %collective-permute-start.3 = (f32[3,512]{1,0:T(4,128)S(1)}, f32[3,512]{1,0:T(4,128)S(1)}, u32[]{:S(2)}, u32[]{:S(2)}) collective-permute-start(f32[3,512]{1,0:T(4,128)S(1)} %pad_maximum_fusion), channel_id=1, source_target_pairs={{0,1},{1,0},{2,3},{3,2},{4,5},{5,4},{6,7},{7,6},{8,9},{9,8},{10,11... | collective-permute-start | bytes 18440 | tf_op jit(solution)/shard_map/ppermute | solution.py:63
  107.2 39.1 %all-to-all-start.6 = ((bf16[8,256,256]{2,1,0:T(8,128)(2,1)}), bf16[8,256,256]{2,1,0:T(8,128)(2,1)S(1)}, u32[]{:S(2)}, u32[]{:S(2)}) async-start(bf16[8,256,256]{2,1,0:T(8,128)(2,1)} %bitcast.127), calls=%async_computation.6 | async-start | bytes 2097152 | tf_op jit(solution)/shard_map/all_to_all | solution.py:74
  179.4 3.9 %collective-permute-start.4 = (f32[3,512]{1,0:T(4,128)S(1)}, f32[3,512]{1,0:T(4,128)S(1)}, u32[]{:S(2)}, u32[]{:S(2)}) collective-permute-start(f32[3,512]{1,0:T(4,128)S(1)} %pad_maximum_fusion.2), channel_id=1, source_target_pairs={{0,1},{1,0},{2,3},{3,2},{4,5},{5,4},{6,7},{7,6},{8,9},{9,8},{10,11... | collective-permute-start | bytes 18440 | tf_op jit(solution)/shard_map/ppermute | solution.py:63
  201.3 32.6 %all-to-all-start.9 = ((bf16[8,256,256]{2,1,0:T(8,128)(2,1)}), bf16[8,256,256]{2,1,0:T(8,128)(2,1)S(1)}, u32[]{:S(2)}, u32[]{:S(2)}) async-start(bf16[8,256,256]{2,1,0:T(8,128)(2,1)} %bitcast.28), calls=%async_computation.9 | async-start | bytes 2097152 | tf_op jit(solution)/shard_map/all_to_all | solution.py:74

commit v3 on v2

--- a/solution.py
+++ b/solution.py
@@ -36,40 +36,44 @@
 
 def shards(features, basis, weights, labels):
     basis_rows = ring(basis, "x", X)
-    image_rows = spread(spread(features, "y", Y), "c", C).reshape(C * Y * 8, FEAT)
-    rolled = jnp.concatenate([
-        lax.dot_general(rows, image_rows, (((1,), (1,)), ((), ())), preferred_element_type=jnp.float32)
-        for rows in basis_rows
-    ])
-    block = in_order(rolled.astype(jnp.bfloat16), "x", X)
-    blocks = spread(spread(spread(block, "y", Y), "x", X), "c", C)
-    blocks = blocks.reshape(C, X, Y, 4, 32, 128)
-    white_t = blocks.transpose(2, 3, 0, 4, 1, 5).reshape(WHITE, 512)
-    labels = labels.reshape(Y, X, C, 8).transpose(1, 2, 0, 3).reshape(512)
+    own_images = spread(features, "y", Y).reshape(Y * 8, FEAT)
+    other_images = lax.ppermute(own_images, "c", [(0, 1), (1, 0)])
+    first = lax.axis_index("c") == 0
+    own_part, other_part = [
+        jnp.concatenate([
+            lax.dot_general(rows, images, (((1,), (1,)), ((), ())), preferred_element_type=jnp.float32)
+            for rows in basis_rows
+        ])
+        for images in (own_images, other_images)
+    ]
+    in_turn = jnp.where(first, own_part, other_part), jnp.where(first, other_part, own_part)
+    block = in_order(jnp.concatenate(in_turn, axis=1).astype(jnp.bfloat16), "x", X)
+    own = spread(spread(block, "y", Y), "x", X).reshape(X, Y, 4, 32, 128)
+    other = lax.ppermute(own, "c", [(0, 1), (1, 0)])
+    white_t = jnp.stack([jnp.where(first, own, other), jnp.where(first, other, own)], axis=3).reshape(X, WHITE, 128)
+    labels = labels.reshape(Y, X, C, 8).transpose(1, 2, 0, 3).reshape(X, 128)
 
     width = weights.shape[1]
     class_ids = lax.axis_index(CLS) * width + lax.iota(jnp.int32, width)
-    target = class_ids[:, None] == labels[None, :]
+    target = labels[:, :, None] == class_ids[None, None, :]
     step_size = STEP_SCALE / WHITE
 
     def forward(current):
         logits = lax.dot_general(
-            current, white_t, (((0,), (0,)), ((), ())), preferred_element_type=jnp.float32
+            white_t, current, (((1,), (0,)), ((), ())), preferred_element_type=jnp.float32
         )
-        picked = jnp.sum(jnp.where(target, logits, 0.0), axis=0)
-        own_top = jnp.max(logits, axis=0)
-        own_total = jnp.sum(jnp.exp(logits - own_top[None]), axis=0)
+        picked = jnp.sum(jnp.where(target, logits, 0.0), axis=2)
+        own_top = jnp.max(logits, axis=2)
+        own_total = jnp.sum(jnp.exp(logits - own_top[:, :, None]), axis=2)
         own = jnp.stack([own_top, own_total, picked])
-        other = lax.ppermute(own, "c", [(0, 1), (1, 0)])
-        first = lax.axis_index("c") == 0
-        pair = joined(jnp.stack([jnp.where(first, own, other), jnp.where(first, other, own)]))
-        parts = spread(jnp.stack(pair).reshape(12, 128), ("y", "x"), Y * X)
-        top, total, label_logit = joined(parts.reshape(Y * X, 3, 512))
+        near = joined(spread(own, ("x", "c"), X * C))
+        far = spread(jnp.stack(near), "y", Y)
+        top, total, label_logit = joined(far)
         losses = top + jnp.log(total) - label_logit
-        probs = jnp.exp(logits - top[None]) / total[None]
+        probs = jnp.exp(logits - top[:, :, None]) / total[:, :, None]
         residue = (probs - target.astype(jnp.float32)).astype(jnp.bfloat16)
         partial = lax.dot_general(
-            white_t, residue, (((1,), (1,)), ((), ())), preferred_element_type=jnp.float32
+            white_t, residue, (((0, 2), (0, 1)), ((), ())), preferred_element_type=jnp.float32
         ).astype(jnp.bfloat16)
         pieces = lax.all_to_all(partial.reshape(Z, WHITE // Z, width), "z", 0, 0, tiled=True)
         return losses, jnp.sum(pieces.astype(jnp.float32), axis=0)

time: 236 us -> 227 us (0.962)
  waiting for transfers between devices: 84.6 us -> 70 us
  blocking collectives: 89.5 us -> 98.3 us
  local copies, waits for them, and re-layouts: 7.99 us -> 4.59 us
    all_to_all x2 -> x1, waiting for transfers between devices: 25.8 us -> 11.7 us  [spread(): return lax.all_to_all(copies, axis, 0, 0, tiled=True)]
    all_to_all x6 -> x7, blocking collectives: 89.5 us -> 98.3 us  [spread(): return lax.all_to_all(copies, axis, 0, 0, tiled=True)]
    all_to_all x2 -> x1, starting transfers between devices: 12.8 us -> 7.65 us  [spread(): return lax.all_to_all(copies, axis, 0, 0, tiled=True)]
    ppermute x2, starting transfers between devices: 5.36 us -> 10.2 us  [the longest x1 5.23 us: shards(): other = lax.ppermute(own, 'c', [(0, 1), (1, 0)])]
    transpose x2 -> x1, local copies, waits for them, and re-layouts: 2.72 us -> 0.01 us  [shards(): labels = labels.reshape(Y, X, C, 8).transpose(1, 2, 0, 3).reshape(X, 128)]
    dot_general x8 -> x12, matrix products: 7.72 us -> 8.21 us  [the longest x2 3.9 us: forward(): lax.dot_general(white_t, residue, (((0, 2), (0, 1)), ((), ())), preferred...]
  transfers between devices with their start and end apart: 9 -> 8, of which waited for: 6 -> 6; matrix products, arithmetic and copies ran while one was open for 1% -> 1% of each run, Pallas kernels for 0% -> 0%
where the time goes in v3:
time: 227 us; the launch traced here: 226 us
  blocking collectives  98.3 us (43%)
  waiting for transfers between devices  70 us (31%)
  starting transfers between devices  40.8 us (18%)
  matrix products  8.21 us (4%)
  local copies, waits for them, and re-layouts  4.59 us (2%)
  other arithmetic  3.63 us (2%)
    all_to_all x7, blocking collectives, spread(): return lax.all_to_all(copies, axis, 0, 0, tiled=True)  98.3 us
    all_to_all x2, waiting for transfers between devices, forward(): lax.all_to_all(partial.reshape(Z, WHITE // Z, width), 'z', 0, 0, tiled=True)  55.8 us
    all_to_all x2, starting transfers between devices, forward(): lax.all_to_all(partial.reshape(Z, WHITE // Z, width), 'z', 0, 0, tiled=True)  13.6 us
    all_to_all x1, waiting for transfers between devices, spread(): return lax.all_to_all(copies, axis, 0, 0, tiled=True)  11.7 us
    ppermute x3, starting transfers between devices, ring(): return [block] + [lax.ppermute(block, axis, pairs) for pairs in back]  9.33 us
    all_to_all x1, starting transfers between devices, spread(): return lax.all_to_all(copies, axis, 0, 0, tiled=True)  7.65 us
    ppermute x1, starting transfers between devices, shards(): other = lax.ppermute(own, 'c', [(0, 1), (1, 0)])  5.23 us
    ppermute x1, starting transfers between devices, shards(): other_images = lax.ppermute(own_images, 'c', [(0, 1), (1, 0)])  4.99 us
  transfers between devices with their start and end apart: 8, of which 6 were waited for; matrix products, arithmetic and copies ran while one was open for 1% of the time, Pallas kernels for 0%

profile of v3, /device:TPU:1, one launch (start us, length us, event | category | flops | bytes accessed | tf_op | source)
XLA Modules:
  0.0 226.5 jit_solution(13092159640871306526)
XLA Ops:
  0.6 1.9 broadcast_in_dim.21
  2.5 7.7 %all-to-all-start = ((bf16[8,8,6144]{2,1,0:T(8,128)(2,1)}), bf16[8,8,6144]{2,1,0:T(8,128)(2,1)S(1)}, u32[]{:S(2)}, u32[]{:S(2)}) async-start(bf16[8,8,6144]{2,1,0:T(8,128)(2,1)} %broadcast_in_dim.21), calls=%async_computation | async-start | bytes 1572864 | tf_op jit(solution)/shard_map/all_to_all | solution.py:16
  10.2 4.4 %collective-permute-start = (bf16[32,6144]{1,0:T(8,128)(2,1)S(1)}, bf16[32,6144]{1,0:T(8,128)(2,1)S(1)}, u32[]{:S(2)}, u32[]{:S(2)}) collective-permute-start(bf16[32,6144]{1,0:T(8,128)(2,1)S(1)} %copy-done), channel_id=1, source_target_pairs={{0,6},{2,0},{4,2},{6,4},{1,7},{3,1},{5,3},{7,5},{8,14},{10,8},{12,... | collective-permute-start | bytes 1179656 | tf_op jit(solution)/shard_map/ppermute | solution.py:21
  14.6 2.4 %collective-permute-start.1 = (bf16[32,6144]{1,0:T(8,128)(2,1)S(1)}, bf16[32,6144]{1,0:T(8,128)(2,1)S(1)}, u32[]{:S(2)}, u32[]{:S(2)}) collective-permute-start(bf16[32,6144]{1,0:T(8,128)(2,1)S(1)} %copy-done), channel_id=1, source_target_pairs={{0,4},{2,6},{4,0},{6,2},{1,5},{3,7},{5,1},{7,3},{8,12},{10,14},{12... | collective-permute-start | bytes 1179656 | tf_op jit(solution)/shard_map/ppermute | solution.py:21
  17.0 2.5 %collective-permute-start.2 = (bf16[32,6144]{1,0:T(8,128)(2,1)S(1)}, bf16[32,6144]{1,0:T(8,128)(2,1)S(1)}, u32[]{:S(2)}, u32[]{:S(2)}) collective-permute-start(bf16[32,6144]{1,0:T(8,128)(2,1)S(1)} %copy-done), channel_id=1, source_target_pairs={{0,2},{2,4},{4,6},{6,0},{1,3},{3,5},{5,7},{7,1},{8,10},{10,12},{12... | collective-permute-start | bytes 1179656 | tf_op jit(solution)/shard_map/ppermute | solution.py:21
  19.5 11.7 %all-to-all-done = bf16[8,8,6144]{2,1,0:T(8,128)(2,1)S(1)} async-done(((bf16[8,8,6144]{2,1,0:T(8,128)(2,1)}), bf16[8,8,6144]{2,1,0:T(8,128)(2,1)S(1)}, u32[]{:S(2)}, u32[]{:S(2)}) %all-to-all-start) | async-done | bytes 786464 | tf_op jit(solution)/shard_map/all_to_all | solution.py:16
  31.2 5.0 %collective-permute-start.3 = (bf16[64,6144]{1,0:T(8,128)(2,1)S(1)}, bf16[64,6144]{1,0:T(8,128)(2,1)S(1)}, u32[]{:S(2)}, u32[]{:S(2)}) collective-permute-start(bf16[64,6144]{1,0:T(8,128)(2,1)S(1)} %bitcast.127), channel_id=1, source_target_pairs={{0,1},{1,0},{2,3},{3,2},{4,5},{5,4},{6,7},{7,6},{8,9},{9,8},{10,11... | collective-permute-start | bytes 2359304 | tf_op jit(solution)/shard_map/ppermute | solution.py:40
  36.2 0.3 fusion.41
  36.5 0.3 fusion.39
  36.9 0.3 fusion.37
  37.2 0.2 collective-permute-done.2
  37.4 0.3 fusion.35
  37.7 0.3 collective-permute-done.3
  38.1 0.3 fusion.48
  38.4 0.3 fusion.47
  38.7 0.3 fusion.46
  39.1 0.3 fusion.45
  39.5 0.2 fusion.21
  39.7 16.8 %all_to_all.50 = bf16[8,128,128]{2,1,0:T(8,128)(2,1)S(1)} all-to-all(bf16[8,128,128]{2,1,0:T(8,128)(2,1)S(1)} %broadcast_in_dim.22), channel_id=1, replica_groups=mesh['z'=8,'y'=8,'x'=4,'c'=2] {'y'}, dimensions={0} | all-to-all | bytes 524288 | tf_op jit(solution)/shard_map/all_to_all | solution.py:16
  56.6 0.2 broadcast_in_dim.23
  56.8 15.1 %all_to_all.51 = bf16[4,8,128,128]{3,2,1,0:T(8,128)(2,1)S(1)} all-to-all(bf16[4,8,128,128]{3,2,1,0:T(8,128)(2,1)S(1)} %broadcast_in_dim.23), channel_id=1, replica_groups=mesh['z'=8,'y'=8,'x'=4,'c'=2] {'x'}, dimensions={0} | all-to-all | bytes 2097152 | tf_op jit(solution)/shard_map/all_to_all | solution.py:16
  71.9 5.2 %collective-permute-start.4 = (bf16[4,8,4,32,128]{4,3,2,1,0:T(8,128)(2,1)S(1)}, bf16[4,8,4,32,128]{4,3,2,1,0:T(8,128)(2,1)S(1)}, u32[]{:S(2)}, u32[]{:S(2)}) collective-permute-start(bf16[4,8,4,32,128]{4,3,2,1,0:T(8,128)(2,1)S(1)} %bitcast.132), channel_id=1, source_target_pairs={{0,1},{1,0},{2,3},{3,2},{4,5},{5,4},{6,7},{7,6},{8,9},{9,8},{10,11... | collective-permute-start | bytes 3145736 | tf_op jit(solution)/shard_map/ppermute | solution.py:52
  77.2 0.1 reshape.129
  77.4 2.0 collective-permute-done.4
  79.4 0.1 select_bitcast_fusion.1
  79.6 0.2 pad_maximum_fusion
  79.8 0.6 copy.40
  80.4 0.6 copy-done.1
  81.0 0.8 fusion.43
  81.9 0.4 exponential_reduce_fusion.1
  82.3 7.5 %all_to_all.52 = f32[8,3,4,128]{3,2,1,0:T(4,128)S(1)} all-to-all(f32[8,3,4,128]{3,2,1,0:T(4,128)S(1)} %broadcast_in_dim.25), channel_id=1, replica_groups=mesh['z'=8,'y'=8,'x'=4,'c'=2] {'x','c'}, dimensions={0} | all-to-all | bytes 98304 | tf_op jit(solution)/shard_map/all_to_all | solution.py:16
  89.9 9.4 %all_to_all.53 = f32[8,3,4,128]{3,2,1,0:T(4,128)S(1)} all-to-all(f32[8,3,4,128]{3,2,1,0:T(4,128)S(1)} %broadcast_in_dim.26), channel_id=1, replica_groups=mesh['z'=8,'y'=8,'x'=4,'c'=2] {'y'}, dimensions={0} | all-to-all | bytes 98304 | tf_op jit(solution)/shard_map/all_to_all | solution.py:16
  99.4 1.9 fusion
  101.3 10.0 %all-to-all-start.5 = ((bf16[8,256,256]{2,1,0:T(8,128)(2,1)}), bf16[8,256,256]{2,1,0:T(8,128)(2,1)S(1)}, u32[]{:S(2)}, u32[]{:S(2)}) async-start(bf16[8,256,256]{2,1,0:T(8,128)(2,1)} %bitcast.135), calls=%async_computation.5 | async-start | bytes 2097152 | tf_op jit(solution)/shard_map/all_to_all | solution.py:78
  111.4 27.7 %all-to-all-done.5 = bf16[8,256,256]{2,1,0:T(8,128)(2,1)S(1)} async-done(((bf16[8,256,256]{2,1,0:T(8,128)(2,1)}), bf16[8,256,256]{2,1,0:T(8,128)(2,1)S(1)}, u32[]{:S(2)}, u32[]{:S(2)}) %all-to-all-start.5) | async-done | bytes 1048608 | tf_op jit(solution)/shard_map/all_to_all | solution.py:78
  139.1 0.1 convert_reduce_fusion.1
  139.2 0.9 subtract_convert_fusion
  140.2 28.3 %all_to_all.54 = bf16[8,256,256]{2,1,0:T(8,128)(2,1)S(1)} all-to-all(bf16[8,256,256]{2,1,0:T(8,128)(2,1)S(1)} %broadcast_in_dim.27), channel_id=1, replica_groups=mesh['z'=8,'y'=8,'x'=4,'c'=2] {'z'}, dimensions={0} | all-to-all | bytes 2097152 | tf_op jit(solution)/shard_map/all_to_all | solution.py:16
  168.5 0.8 fusion.44
  169.4 0.4 exponential_reduce_fusion
  169.8 10.9 %all_to_all.55 = f32[8,3,4,128]{3,2,1,0:T(4,128)S(1)} all-to-all(f32[8,3,4,128]{3,2,1,0:T(4,128)S(1)} %broadcast_in_dim.28), channel_id=1, replica_groups=mesh['z'=8,'y'=8,'x'=4,'c'=2] {'x','c'}, dimensions={0} | all-to-all | bytes 98304 | tf_op jit(solution)/shard_map/all_to_all | solution.py:16
  180.8 10.1 %all_to_all.56 = f32[8,3,4,128]{3,2,1,0:T(4,128)S(1)} all-to-all(f32[8,3,4,128]{3,2,1,0:T(4,128)S(1)} %broadcast_in_dim.29), channel_id=1, replica_groups=mesh['z'=8,'y'=8,'x'=4,'c'=2] {'y'}, dimensions={0} | all-to-all | bytes 98304 | tf_op jit(solution)/shard_map/all_to_all | solution.py:16
  191.0 1.9 fusion.1
  192.9 3.6 %all-to-all-start.9 = ((bf16[8,256,256]{2,1,0:T(8,128)(2,1)}), bf16[8,256,256]{2,1,0:T(8,128)(2,1)S(1)}, u32[]{:S(2)}, u32[]{:S(2)}) async-start(bf16[8,256,256]{2,1,0:T(8,128)(2,1)} %bitcast.33), calls=%async_computation.9 | async-start | bytes 2097152 | tf_op jit(solution)/shard_map/all_to_all | solution.py:78
  196.8 0.7 reshape.132
  197.5 28.1 %all-to-all-done.9 = bf16[8,256,256]{2,1,0:T(8,128)(2,1)S(1)} async-done(((bf16[8,256,256]{2,1,0:T(8,128)(2,1)}), bf16[8,256,256]{2,1,0:T(8,128)(2,1)S(1)}, u32[]{:S(2)}, u32[]{:S(2)}) %all-to-all-start.9) | async-done | bytes 1048608 | tf_op jit(solution)/shard_map/all_to_all | solution.py:78
  225.6 0.1 convert_reduce_fusion
  225.8 0.7 add.57
  (39 shorter events, 0.8 us)
Async XLA Ops:
  0.6 9.5 %copy-start = (bf16[32,6144]{1,0:T(8,128)(2,1)S(1)}, bf16[32,6144]{1,0:T(8,128)(2,1)}, u32[]{:S(2)}) copy-start(bf16[32,6144]{1,0:T(8,128)(2,1)} %param.5) | copy-start | bytes 1179652
  2.5 28.7 %all-to-all-start = ((bf16[8,8,6144]{2,1,0:T(8,128)(2,1)}), bf16[8,8,6144]{2,1,0:T(8,128)(2,1)S(1)}, u32[]{:S(2)}, u32[]{:S(2)}) async-start(bf16[8,8,6144]{2,1,0:T(8,128)(2,1)} %broadcast_in_dim.21), calls=%async_computation | async-start | bytes 1572864 | tf_op jit(solution)/shard_map/all_to_all | solution.py:16
  10.2 26.4 %collective-permute-start = (bf16[32,6144]{1,0:T(8,128)(2,1)S(1)}, bf16[32,6144]{1,0:T(8,128)(2,1)S(1)}, u32[]{:S(2)}, u32[]{:S(2)}) collective-permute-start(bf16[32,6144]{1,0:T(8,128)(2,1)S(1)} %copy-done), channel_id=1, source_target_pairs={{0,6},{2,0},{4,2},{6,4},{1,7},{3,1},{5,3},{7,5},{8,14},{10,8},{12,... | collective-permute-start | bytes 1179656 | tf_op jit(solution)/shard_map/ppermute | solution.py:21
  14.6 22.3 %collective-permute-start.1 = (bf16[32,6144]{1,0:T(8,128)(2,1)S(1)}, bf16[32,6144]{1,0:T(8,128)(2,1)S(1)}, u32[]{:S(2)}, u32[]{:S(2)}) collective-permute-start(bf16[32,6144]{1,0:T(8,128)(2,1)S(1)} %copy-done), channel_id=1, source_target_pairs={{0,4},{2,6},{4,0},{6,2},{1,5},{3,7},{5,1},{7,3},{8,12},{10,14},{12... | collective-permute-start | bytes 1179656 | tf_op jit(solution)/shard_map/ppermute | solution.py:21
  17.0 20.4 %collective-permute-start.2 = (bf16[32,6144]{1,0:T(8,128)(2,1)S(1)}, bf16[32,6144]{1,0:T(8,128)(2,1)S(1)}, u32[]{:S(2)}, u32[]{:S(2)}) collective-permute-start(bf16[32,6144]{1,0:T(8,128)(2,1)S(1)} %copy-done), channel_id=1, source_target_pairs={{0,2},{2,4},{4,6},{6,0},{1,3},{3,5},{5,7},{7,1},{8,10},{10,12},{12... | collective-permute-start | bytes 1179656 | tf_op jit(solution)/shard_map/ppermute | solution.py:21
  31.2 6.9 %collective-permute-start.3 = (bf16[64,6144]{1,0:T(8,128)(2,1)S(1)}, bf16[64,6144]{1,0:T(8,128)(2,1)S(1)}, u32[]{:S(2)}, u32[]{:S(2)}) collective-permute-start(bf16[64,6144]{1,0:T(8,128)(2,1)S(1)} %bitcast.127), channel_id=1, source_target_pairs={{0,1},{1,0},{2,3},{3,2},{4,5},{5,4},{6,7},{7,6},{8,9},{9,8},{10,11... | collective-permute-start | bytes 2359304 | tf_op jit(solution)/shard_map/ppermute | solution.py:40
  39.7 37.5 %copy-start.2 = (s32[512]{0:T(512)S(1)}, s32[512]{0:T(512)}, u32[]{:S(2)}) copy-start(s32[512]{0:T(512)} %param.7) | copy-start | bytes 6148
  71.9 7.5 %collective-permute-start.4 = (bf16[4,8,4,32,128]{4,3,2,1,0:T(8,128)(2,1)S(1)}, bf16[4,8,4,32,128]{4,3,2,1,0:T(8,128)(2,1)S(1)}, u32[]{:S(2)}, u32[]{:S(2)}) collective-permute-start(bf16[4,8,4,32,128]{4,3,2,1,0:T(8,128)(2,1)S(1)} %bitcast.132), channel_id=1, source_target_pairs={{0,1},{1,0},{2,3},{3,2},{4,5},{5,4},{6,7},{7,6},{8,9},{9,8},{10,11... | collective-permute-start | bytes 3145736 | tf_op jit(solution)/shard_map/ppermute | solution.py:52
  79.8 1.2 copy-start.1
  101.3 37.8 %all-to-all-start.5 = ((bf16[8,256,256]{2,1,0:T(8,128)(2,1)}), bf16[8,256,256]{2,1,0:T(8,128)(2,1)S(1)}, u32[]{:S(2)}, u32[]{:S(2)}) async-start(bf16[8,256,256]{2,1,0:T(8,128)(2,1)} %bitcast.135), calls=%async_computation.5 | async-start | bytes 2097152 | tf_op jit(solution)/shard_map/all_to_all | solution.py:78
  192.9 32.7 %all-to-all-start.9 = ((bf16[8,256,256]{2,1,0:T(8,128)(2,1)}), bf16[8,256,256]{2,1,0:T(8,128)(2,1)S(1)}, u32[]{:S(2)}, u32[]{:S(2)}) async-start(bf16[8,256,256]{2,1,0:T(8,128)(2,1)} %bitcast.33), calls=%async_computation.9 | async-start | bytes 2097152 | tf_op jit(solution)/shard_map/all_to_all | solution.py:78

commit v4 on v3

--- a/solution.py
+++ b/solution.py
@@ -7,7 +7,9 @@
 FEAT = 6144
 WHITE = 2048
 STEP_SCALE = 2.0
-Z, Y, X, C = 8, 8, 4, 2
+ZH, ZL, Y, X, C = 4, 2, 8, 4, 2
+Z = ZH * ZL
+DP = ("zh", "zl")
 CLS = ("y", "x", "c")
 
 
@@ -51,6 +53,11 @@
     own = spread(spread(block, "y", Y), "x", X).reshape(X, Y, 4, 32, 128)
     other = lax.ppermute(own, "c", [(0, 1), (1, 0)])
     white_t = jnp.stack([jnp.where(first, own, other), jnp.where(first, other, own)], axis=3).reshape(X, WHITE, 128)
+    parity = lax.axis_index("zl")
+    white_near, white_far = [
+        lax.dynamic_index_in_dim(white_t.reshape(X, ZH, ZL, WHITE // Z, 128), which, 2, keepdims=False).reshape(X, WHITE // 2, 128)
+        for which in (parity, 1 - parity)
+    ]
     labels = labels.reshape(Y, X, C, 8).transpose(1, 2, 0, 3).reshape(X, 128)
 
     width = weights.shape[1]
@@ -58,10 +65,10 @@
     target = labels[:, :, None] == class_ids[None, None, :]
     step_size = STEP_SCALE / WHITE
 
-    def forward(current):
-        logits = lax.dot_general(
-            white_t, current, (((1,), (0,)), ((), ())), preferred_element_type=jnp.float32
-        )
+    def product(white, current):
+        return lax.dot_general(white, current, (((1,), (0,)), ((), ())), preferred_element_type=jnp.float32)
+
+    def forward(logits):
         picked = jnp.sum(jnp.where(target, logits, 0.0), axis=2)
         own_top = jnp.max(logits, axis=2)
         own_total = jnp.sum(jnp.exp(logits - own_top[:, :, None]), axis=2)
@@ -75,21 +82,26 @@
         partial = lax.dot_general(
             white_t, residue, (((0, 2), (0, 1)), ((), ())), preferred_element_type=jnp.float32
         ).astype(jnp.bfloat16)
-        pieces = lax.all_to_all(partial.reshape(Z, WHITE // Z, width), "z", 0, 0, tiled=True)
+        pieces = lax.all_to_all(partial.reshape(Z, WHITE // Z, width), DP, 0, 0, tiled=True)
         return losses, jnp.sum(pieces.astype(jnp.float32), axis=0)
 
-    losses_first, grad_first = forward(weights)
-    own_rows = lax.dynamic_slice_in_dim(weights, lax.axis_index("z") * (WHITE // Z), WHITE // Z, 0)
+    losses_first, grad_first = forward(product(white_t, weights))
+    own_rows = lax.dynamic_slice_in_dim(weights, lax.axis_index(DP) * (WHITE // Z), WHITE // Z, 0)
     own_updated = (own_rows.astype(jnp.float32) - step_size * grad_first).astype(jnp.bfloat16)
-    updated = spread(own_updated, "z", Z).reshape(WHITE, width)
-    losses_second, grad_second = forward(updated)
+    half = width // 2
+    near = spread(own_updated, "zh", ZH).reshape(WHITE // 2, width)
+    ahead = lax.ppermute(near[:, :half], DP, [(at, (at - 1) % Z) for at in range(Z)])
+    behind = lax.ppermute(near[:, half:], DP, [(at, (at + 1) % Z) for at in range(Z)])
+    logits = product(white_near, near)
+    logits = logits + jnp.concatenate([product(white_far, ahead), product(white_far, behind)], axis=2)
+    losses_second, grad_second = forward(logits)
     losses = jnp.stack([losses_first, losses_second])
     losses = losses.reshape(2, X, C, Y, 8).transpose(0, 3, 1, 2, 4).reshape(2, 512)
     return losses, grad_first + grad_second
 
 
 def solution(mesh):
-    fine = Mesh(mesh.devices.reshape(Z, Y, X, C), ("z", "y", "x", "c"))
-    in_specs = (P(("z",) + CLS, None), P(CLS, None), P(None, CLS), P("z"))
-    out_specs = (P(None, "z"), P("z", CLS))
+    fine = Mesh(mesh.devices.reshape(ZH, ZL, Y, X, C), DP + CLS)
+    in_specs = (P(DP + CLS, None), P(CLS, None), P(None, CLS), P(DP))
+    out_specs = (P(None, DP), P(DP, CLS))
     return jax.shard_map(shards, mesh=fine, in_specs=in_specs, out_specs=out_specs, check_vma=False)

time: 227 us -> 225 us (level)
  blocking collectives: 98.3 us -> 86.1 us
  starting transfers between devices: 40.8 us -> 48.4 us
    all_to_all x7, blocking collectives: 98.3 us -> 86.1 us  [spread(): return lax.all_to_all(copies, axis, 0, 0, tiled=True)]
    ppermute x0 -> x2, starting transfers between devices: none -> 6.49 us  [the longest x1 4.57 us: shards(): lax.ppermute(near[:, :half], DP, [(at, (at - 1) % Z) for at in range(Z)])]
  transfers between devices with their start and end apart: 8 -> 10, of which waited for: 6 -> 8; matrix products, arithmetic and copies ran while one was open for 1% -> 2% of each run, Pallas kernels for 0% -> 0%
where the time goes in v4:
time: 225 us; the launch traced here: 224 us
  blocking collectives  86.1 us (38%)
  waiting for transfers between devices  70.2 us (31%)
  starting transfers between devices  48.4 us (22%)
  matrix products  9.85 us (4%)
  local copies, waits for them, and re-layouts  4.75 us (2%)
  other arithmetic  3.63 us (2%)
    all_to_all x7, blocking collectives, spread(): return lax.all_to_all(copies, axis, 0, 0, tiled=True)  86.1 us
    all_to_all x2, waiting for transfers between devices, forward(): lax.all_to_all(partial.reshape(Z, WHITE // Z, width), DP, 0, 0, tiled=True)  54.1 us
    all_to_all x2, starting transfers between devices, forward(): lax.all_to_all(partial.reshape(Z, WHITE // Z, width), DP, 0, 0, tiled=True)  14.7 us
    all_to_all x1, waiting for transfers between devices, spread(): return lax.all_to_all(copies, axis, 0, 0, tiled=True)  11.7 us
    ppermute x3, starting transfers between devices, ring(): return [block] + [lax.ppermute(block, axis, pairs) for pairs in back]  9.33 us
    all_to_all x1, starting transfers between devices, spread(): return lax.all_to_all(copies, axis, 0, 0, tiled=True)  7.65 us
    ppermute x1, starting transfers between devices, shards(): other = lax.ppermute(own, 'c', [(0, 1), (1, 0)])  5.23 us
    ppermute x1, starting transfers between devices, shards(): other_images = lax.ppermute(own_images, 'c', [(0, 1), (1, 0)])  4.99 us
  transfers between devices with their start and end apart: 10, of which 8 were waited for; matrix products, arithmetic and copies ran while one was open for 2% of the time, Pallas kernels for 0%

profile of v4, /device:TPU:1, one launch (start us, length us, event | category | flops | bytes accessed | tf_op | source)
XLA Modules:
  0.0 223.9 jit_solution(17834763293873562479)
XLA Ops:
  0.6 1.9 broadcast_in_dim.21
  2.5 7.7 %all-to-all-start = ((bf16[8,8,6144]{2,1,0:T(8,128)(2,1)}), bf16[8,8,6144]{2,1,0:T(8,128)(2,1)S(1)}, u32[]{:S(2)}, u32[]{:S(2)}) async-start(bf16[8,8,6144]{2,1,0:T(8,128)(2,1)} %broadcast_in_dim.21), calls=%async_computation | async-start | bytes 1572864 | tf_op jit(solution)/shard_map/all_to_all | solution.py:18
  10.2 4.4 %collective-permute-start = (bf16[32,6144]{1,0:T(8,128)(2,1)S(1)}, bf16[32,6144]{1,0:T(8,128)(2,1)S(1)}, u32[]{:S(2)}, u32[]{:S(2)}) collective-permute-start(bf16[32,6144]{1,0:T(8,128)(2,1)S(1)} %copy-done), channel_id=1, source_target_pairs={{0,6},{2,0},{4,2},{6,4},{1,7},{3,1},{5,3},{7,5},{8,14},{10,8},{12,... | collective-permute-start | bytes 1179656 | tf_op jit(solution)/shard_map/ppermute | solution.py:23
  14.6 2.4 %collective-permute-start.1 = (bf16[32,6144]{1,0:T(8,128)(2,1)S(1)}, bf16[32,6144]{1,0:T(8,128)(2,1)S(1)}, u32[]{:S(2)}, u32[]{:S(2)}) collective-permute-start(bf16[32,6144]{1,0:T(8,128)(2,1)S(1)} %copy-done), channel_id=1, source_target_pairs={{0,4},{2,6},{4,0},{6,2},{1,5},{3,7},{5,1},{7,3},{8,12},{10,14},{12... | collective-permute-start | bytes 1179656 | tf_op jit(solution)/shard_map/ppermute | solution.py:23
  17.0 2.5 %collective-permute-start.2 = (bf16[32,6144]{1,0:T(8,128)(2,1)S(1)}, bf16[32,6144]{1,0:T(8,128)(2,1)S(1)}, u32[]{:S(2)}, u32[]{:S(2)}) collective-permute-start(bf16[32,6144]{1,0:T(8,128)(2,1)S(1)} %copy-done), channel_id=1, source_target_pairs={{0,2},{2,4},{4,6},{6,0},{1,3},{3,5},{5,7},{7,1},{8,10},{10,12},{12... | collective-permute-start | bytes 1179656 | tf_op jit(solution)/shard_map/ppermute | solution.py:23
  19.5 11.7 %all-to-all-done = bf16[8,8,6144]{2,1,0:T(8,128)(2,1)S(1)} async-done(((bf16[8,8,6144]{2,1,0:T(8,128)(2,1)}), bf16[8,8,6144]{2,1,0:T(8,128)(2,1)S(1)}, u32[]{:S(2)}, u32[]{:S(2)}) %all-to-all-start) | async-done | bytes 786464 | tf_op jit(solution)/shard_map/all_to_all | solution.py:18
  31.2 5.0 %collective-permute-start.3 = (bf16[64,6144]{1,0:T(8,128)(2,1)S(1)}, bf16[64,6144]{1,0:T(8,128)(2,1)S(1)}, u32[]{:S(2)}, u32[]{:S(2)}) collective-permute-start(bf16[64,6144]{1,0:T(8,128)(2,1)S(1)} %bitcast.138), channel_id=1, source_target_pairs={{0,1},{1,0},{2,3},{3,2},{4,5},{5,4},{6,7},{7,6},{8,9},{9,8},{10,11... | collective-permute-start | bytes 2359304 | tf_op jit(solution)/shard_map/ppermute | solution.py:42
  36.2 0.3 fusion.45
  36.5 0.3 fusion.43
  36.9 0.3 fusion.41
  37.2 0.2 collective-permute-done.2
  37.4 0.3 fusion.39
  37.7 0.3 collective-permute-done.3
  38.1 0.3 fusion.53
  38.4 0.3 fusion.52
  38.7 0.3 fusion.51
  39.1 0.3 fusion.50
  39.5 0.2 fusion.25
  39.7 16.8 %all_to_all.50 = bf16[8,128,128]{2,1,0:T(8,128)(2,1)S(1)} all-to-all(bf16[8,128,128]{2,1,0:T(8,128)(2,1)S(1)} %broadcast_in_dim.22), channel_id=1, replica_groups=mesh['zh'=4,'zl'=2,'y'=8,'x'=4,'c'=2] {'y'}, dimensions={0} | all-to-all | bytes 524288 | tf_op jit(solution)/shard_map/all_to_all | solution.py:18
  56.6 0.2 broadcast_in_dim.23
  56.8 15.1 %all_to_all.51 = bf16[4,8,128,128]{3,2,1,0:T(8,128)(2,1)S(1)} all-to-all(bf16[4,8,128,128]{3,2,1,0:T(8,128)(2,1)S(1)} %broadcast_in_dim.23), channel_id=1, replica_groups=mesh['zh'=4,'zl'=2,'y'=8,'x'=4,'c'=2] {'x'}, dimensions={0} | all-to-all | bytes 2097152 | tf_op jit(solution)/shard_map/all_to_all | solution.py:18
  71.9 5.2 %collective-permute-start.4 = (bf16[4,8,4,32,128]{4,3,2,1,0:T(8,128)(2,1)S(1)}, bf16[4,8,4,32,128]{4,3,2,1,0:T(8,128)(2,1)S(1)}, u32[]{:S(2)}, u32[]{:S(2)}) collective-permute-start(bf16[4,8,4,32,128]{4,3,2,1,0:T(8,128)(2,1)S(1)} %bitcast.147), channel_id=1, source_target_pairs={{0,1},{1,0},{2,3},{3,2},{4,5},{5,4},{6,7},{7,6},{8,9},{9,8},{10,11... | collective-permute-start | bytes 3145736 | tf_op jit(solution)/shard_map/ppermute | solution.py:54
  77.4 2.0 collective-permute-done.4
  79.8 0.6 copy.61
  80.4 0.6 copy-done.1
  81.0 0.8 fusion.49
  81.9 0.4 exponential_reduce_fusion.1
  82.3 7.5 %all_to_all.52 = f32[8,3,4,128]{3,2,1,0:T(4,128)S(1)} all-to-all(f32[8,3,4,128]{3,2,1,0:T(4,128)S(1)} %broadcast_in_dim.25), channel_id=1, replica_groups=mesh['zh'=4,'zl'=2,'y'=8,'x'=4,'c'=2] {'x','c'}, dimensions={0} | all-to-all | bytes 98304 | tf_op jit(solution)/shard_map/all_to_all | solution.py:18
  89.9 9.4 %all_to_all.53 = f32[8,3,4,128]{3,2,1,0:T(4,128)S(1)} all-to-all(f32[8,3,4,128]{3,2,1,0:T(4,128)S(1)} %broadcast_in_dim.26), channel_id=1, replica_groups=mesh['zh'=4,'zl'=2,'y'=8,'x'=4,'c'=2] {'y'}, dimensions={0} | all-to-all | bytes 98304 | tf_op jit(solution)/shard_map/all_to_all | solution.py:18
  99.4 1.9 fusion
  101.3 10.0 %all-to-all-start.5 = ((bf16[8,256,256]{2,1,0:T(8,128)(2,1)}), bf16[8,256,256]{2,1,0:T(8,128)(2,1)S(1)}, u32[]{:S(2)}, u32[]{:S(2)}) async-start(bf16[8,256,256]{2,1,0:T(8,128)(2,1)} %bitcast.150), calls=%async_computation.5 | async-start | bytes 2097152 | tf_op jit(solution)/shard_map/all_to_all | solution.py:85
  111.4 27.7 %all-to-all-done.5 = bf16[8,256,256]{2,1,0:T(8,128)(2,1)S(1)} async-done(((bf16[8,256,256]{2,1,0:T(8,128)(2,1)}), bf16[8,256,256]{2,1,0:T(8,128)(2,1)S(1)}, u32[]{:S(2)}, u32[]{:S(2)}) %all-to-all-start.5) | async-done | bytes 1048608 | tf_op jit(solution)/shard_map/all_to_all | solution.py:85
  139.2 0.9 subtract_convert_fusion
  140.2 14.9 %all_to_all.54 = bf16[4,256,256]{2,1,0:T(8,128)(2,1)S(1)} all-to-all(bf16[4,256,256]{2,1,0:T(8,128)(2,1)S(1)} %broadcast_in_dim.27), channel_id=1, replica_groups=mesh['zh'=4,'zl'=2,'y'=8,'x'=4,'c'=2] {'zh'}, dimensions={0} | all-to-all | bytes 1048576 | tf_op jit(solution)/shard_map/all_to_all | solution.py:18
  155.2 1.9 collective-permute-start.6
  157.3 4.6 %collective-permute-start.5 = (bf16[1024,128]{1,0:T(8,128)(2,1)S(1)}, bf16[1024,128]{1,0:T(8,128)(2,1)S(1)}, u32[]{:S(2)}, u32[]{:S(2)}) collective-permute-start(bf16[1024,128]{1,0:T(8,128)(2,1)S(1)} %get-tuple-element.12), channel_id=1, source_target_pairs={{0,448},{64,0},{128,64},{192,128},{256,192},{320,256},{384,320},{4... | collective-permute-start | bytes 786440 | tf_op jit(solution)/shard_map/ppermute | solution.py:93
  161.9 1.8 collective-permute-done.6
  163.6 1.4 fusion.12
  165.1 0.5 fusion.14
  165.6 0.6 fusion.47
  166.2 0.4 exponential_reduce_fusion
  166.6 11.4 %all_to_all.55 = f32[8,3,4,128]{3,2,1,0:T(4,128)S(1)} all-to-all(f32[8,3,4,128]{3,2,1,0:T(4,128)S(1)} %broadcast_in_dim.28), channel_id=1, replica_groups=mesh['zh'=4,'zl'=2,'y'=8,'x'=4,'c'=2] {'x','c'}, dimensions={0} | all-to-all | bytes 98304 | tf_op jit(solution)/shard_map/all_to_all | solution.py:18
  178.1 10.9 %all_to_all.56 = f32[8,3,4,128]{3,2,1,0:T(4,128)S(1)} all-to-all(f32[8,3,4,128]{3,2,1,0:T(4,128)S(1)} %broadcast_in_dim.29), channel_id=1, replica_groups=mesh['zh'=4,'zl'=2,'y'=8,'x'=4,'c'=2] {'y'}, dimensions={0} | all-to-all | bytes 98304 | tf_op jit(solution)/shard_map/all_to_all | solution.py:18
  189.0 1.9 fusion.1
  190.9 4.7 %all-to-all-start.9 = ((bf16[8,256,256]{2,1,0:T(8,128)(2,1)}), bf16[8,256,256]{2,1,0:T(8,128)(2,1)S(1)}, u32[]{:S(2)}, u32[]{:S(2)}) async-start(bf16[8,256,256]{2,1,0:T(8,128)(2,1)} %bitcast.38), calls=%async_computation.9 | async-start | bytes 2097152 | tf_op jit(solution)/shard_map/all_to_all | solution.py:85
  195.9 0.7 reshape.142
  196.7 26.4 %all-to-all-done.9 = bf16[8,256,256]{2,1,0:T(8,128)(2,1)S(1)} async-done(((bf16[8,256,256]{2,1,0:T(8,128)(2,1)}), bf16[8,256,256]{2,1,0:T(8,128)(2,1)S(1)}, u32[]{:S(2)}, u32[]{:S(2)}) %all-to-all-start.9) | async-done | bytes 1048608 | tf_op jit(solution)/shard_map/all_to_all | solution.py:85
  223.2 0.7 add.75
  (47 shorter events, 1.8 us)
Async XLA Ops:
  0.6 9.5 %copy-start = (bf16[32,6144]{1,0:T(8,128)(2,1)S(1)}, bf16[32,6144]{1,0:T(8,128)(2,1)}, u32[]{:S(2)}) copy-start(bf16[32,6144]{1,0:T(8,128)(2,1)} %param.5) | copy-start | bytes 1179652
  2.5 28.7 %all-to-all-start = ((bf16[8,8,6144]{2,1,0:T(8,128)(2,1)}), bf16[8,8,6144]{2,1,0:T(8,128)(2,1)S(1)}, u32[]{:S(2)}, u32[]{:S(2)}) async-start(bf16[8,8,6144]{2,1,0:T(8,128)(2,1)} %broadcast_in_dim.21), calls=%async_computation | async-start | bytes 1572864 | tf_op jit(solution)/shard_map/all_to_all | solution.py:18
  10.2 26.4 %collective-permute-start = (bf16[32,6144]{1,0:T(8,128)(2,1)S(1)}, bf16[32,6144]{1,0:T(8,128)(2,1)S(1)}, u32[]{:S(2)}, u32[]{:S(2)}) collective-permute-start(bf16[32,6144]{1,0:T(8,128)(2,1)S(1)} %copy-done), channel_id=1, source_target_pairs={{0,6},{2,0},{4,2},{6,4},{1,7},{3,1},{5,3},{7,5},{8,14},{10,8},{12,... | collective-permute-start | bytes 1179656 | tf_op jit(solution)/shard_map/ppermute | solution.py:23
  14.6 22.3 %collective-permute-start.1 = (bf16[32,6144]{1,0:T(8,128)(2,1)S(1)}, bf16[32,6144]{1,0:T(8,128)(2,1)S(1)}, u32[]{:S(2)}, u32[]{:S(2)}) collective-permute-start(bf16[32,6144]{1,0:T(8,128)(2,1)S(1)} %copy-done), channel_id=1, source_target_pairs={{0,4},{2,6},{4,0},{6,2},{1,5},{3,7},{5,1},{7,3},{8,12},{10,14},{12... | collective-permute-start | bytes 1179656 | tf_op jit(solution)/shard_map/ppermute | solution.py:23
  17.0 20.4 %collective-permute-start.2 = (bf16[32,6144]{1,0:T(8,128)(2,1)S(1)}, bf16[32,6144]{1,0:T(8,128)(2,1)S(1)}, u32[]{:S(2)}, u32[]{:S(2)}) collective-permute-start(bf16[32,6144]{1,0:T(8,128)(2,1)S(1)} %copy-done), channel_id=1, source_target_pairs={{0,2},{2,4},{4,6},{6,0},{1,3},{3,5},{5,7},{7,1},{8,10},{10,12},{12... | collective-permute-start | bytes 1179656 | tf_op jit(solution)/shard_map/ppermute | solution.py:23
  31.2 6.9 %collective-permute-start.3 = (bf16[64,6144]{1,0:T(8,128)(2,1)S(1)}, bf16[64,6144]{1,0:T(8,128)(2,1)S(1)}, u32[]{:S(2)}, u32[]{:S(2)}) collective-permute-start(bf16[64,6144]{1,0:T(8,128)(2,1)S(1)} %bitcast.138), channel_id=1, source_target_pairs={{0,1},{1,0},{2,3},{3,2},{4,5},{5,4},{6,7},{7,6},{8,9},{9,8},{10,11... | collective-permute-start | bytes 2359304 | tf_op jit(solution)/shard_map/ppermute | solution.py:42
  39.7 37.5 %copy-start.2 = (s32[512]{0:T(512)S(1)}, s32[512]{0:T(512)}, u32[]{:S(2)}) copy-start(s32[512]{0:T(512)} %param.7) | copy-start | bytes 6148
  71.9 7.5 %collective-permute-start.4 = (bf16[4,8,4,32,128]{4,3,2,1,0:T(8,128)(2,1)S(1)}, bf16[4,8,4,32,128]{4,3,2,1,0:T(8,128)(2,1)S(1)}, u32[]{:S(2)}, u32[]{:S(2)}) collective-permute-start(bf16[4,8,4,32,128]{4,3,2,1,0:T(8,128)(2,1)S(1)} %bitcast.147), channel_id=1, source_target_pairs={{0,1},{1,0},{2,3},{3,2},{4,5},{5,4},{6,7},{7,6},{8,9},{9,8},{10,11... | collective-permute-start | bytes 3145736 | tf_op jit(solution)/shard_map/ppermute | solution.py:54
  79.8 1.2 copy-start.1
  101.3 37.8 %all-to-all-start.5 = ((bf16[8,256,256]{2,1,0:T(8,128)(2,1)}), bf16[8,256,256]{2,1,0:T(8,128)(2,1)S(1)}, u32[]{:S(2)}, u32[]{:S(2)}) async-start(bf16[8,256,256]{2,1,0:T(8,128)(2,1)} %bitcast.150), calls=%async_computation.5 | async-start | bytes 2097152 | tf_op jit(solution)/shard_map/all_to_all | solution.py:85
  155.2 8.4 %collective-permute-start.6 = (bf16[1024,128]{1,0:T(8,128)(2,1)S(1)}, bf16[1024,128]{1,0:T(8,128)(2,1)}, u32[]{:S(2)}, u32[]{:S(2)}) collective-permute-start(bf16[1024,128]{1,0:T(8,128)(2,1)S(1)} %get-tuple-element.13), channel_id=1, source_target_pairs={{0,64},{64,128},{128,192},{192,256},{256,320},{320,384},{384,448},... | collective-permute-start | bytes 786440 | tf_op jit(solution)/shard_map/ppermute | solution.py:94
  157.3 7.9 %collective-permute-start.5 = (bf16[1024,128]{1,0:T(8,128)(2,1)S(1)}, bf16[1024,128]{1,0:T(8,128)(2,1)S(1)}, u32[]{:S(2)}, u32[]{:S(2)}) collective-permute-start(bf16[1024,128]{1,0:T(8,128)(2,1)S(1)} %get-tuple-element.12), channel_id=1, source_target_pairs={{0,448},{64,0},{128,64},{192,128},{256,192},{320,256},{384,320},{4... | collective-permute-start | bytes 786440 | tf_op jit(solution)/shard_map/ppermute | solution.py:93
  190.9 32.1 %all-to-all-start.9 = ((bf16[8,256,256]{2,1,0:T(8,128)(2,1)}), bf16[8,256,256]{2,1,0:T(8,128)(2,1)S(1)}, u32[]{:S(2)}, u32[]{:S(2)}) async-start(bf16[8,256,256]{2,1,0:T(8,128)(2,1)} %bitcast.38), calls=%async_computation.9 | async-start | bytes 2097152 | tf_op jit(solution)/shard_map/all_to_all | solution.py:85
